TPU v7x, 32 devices: a whole 2x2x4 slice. The times are simulated.
32 devices in a mesh: dp: 8 (over z, x), mp: 4 (over y, core).
Axes of the slice: x: 2, y: 2, z: 4, core: 2. Of those that a mesh axis runs over, the one named last changes fastest.
Arguments:
- frames: bfloat16 [128, 30, 4, 84, 84], P(('dp', 'mp')), may hold values from 0 to 1
- returns: float32 [128, 30], P(('dp', 'mp')), may hold values from 0 to 4
- actions: int32 [128, 30], P(('dp', 'mp')), may hold values from 0 to 17
- starts: int32 [128], P(('dp', 'mp')), may hold values from 0 to 4066
- lengths: int32 [128], P(('dp', 'mp')), may hold values from 1 to 30, as said below
- shared_weights: float32 [1010688], replicated
- shared_first: float32 [1010688], replicated, may hold values from -0.00012207031 to 0.00012207031
- shared_second: float32 [1010688], replicated, may hold values from 3.5589012e-10 to 1.4235605e-09
- split_weights: float32 [394240], P('mp')
- split_first: float32 [394240], P('mp'), may hold values from -0.00012207031 to 0.00012207031
- split_second: float32 [394240], P('mp'), may hold values from 3.5589012e-10 to 1.4235605e-09
Outputs:
- shared_new: float32 [1010688], replicated
- shared_first_new: float32 [1010688], replicated
- shared_second_new: float32 [1010688], replicated
- shared_low: bfloat16 [1010688], replicated
- split_new: float32 [394240], P('mp')
- split_first_new: float32 [394240], P('mp')
- split_second_new: float32 [394240], P('mp')
- split_low: bfloat16 [394240], P('mp')
- grad_norm: float32 [], replicated
- loss_sum: float32 [], replicated
- valid_count: float32 [], replicated
Inputs may be any that keep to these rules, and one draw needn't show every extreme that they name: `lengths`: lengths are heavy-tailed and larger on later windows; the last window of all has 30.
All inputs are finite; a program needn't handle non-finite values.
Results may differ from a plain program's by a relative error of at most 0.001.
Values sent between devices are 32-bit elements; how exact they have to be, the bound alone decides.
A program may use at most 192 MiB of HBM per device.

v0:
```python
from functools import partial
import math

import jax
import jax.numpy as jnp
from jax import lax
from jax.experimental import pallas as pl
from jax.experimental.pallas import tpu as pltpu
from jax.sharding import PartitionSpec as P

D = 128
FF = 512
ACT = 18
C1 = 32
C2 = 64
TSTEPS = 4096
LAYERS = 2
STEP = 10
HD = 16


clip_limit = 0.1
learn_rate = 0.05
beta_first = 0.9
beta_second = 0.95
adam_epsilon = 1e-08
weight_decay = 0.1


def span_layout(narrow, hidden):
    return [
        ("qkv", (D, 3, narrow)),
        ("output", (narrow, D)),
        ("up", (D, hidden)),
        ("up_bias", (hidden,)),
        ("down", (hidden, D)),
    ]


def assemble(flat, copies, narrow, hidden):
    layout = span_layout(narrow, hidden)
    width = sum((math.prod(shape) for name, shape in layout))
    blocks = flat.reshape(copies, LAYERS, width)
    layers = []
    for layer in range(LAYERS):
        offset = 0
        pieces = {}
        for name, shape in layout:
            count = math.prod(shape)
            pieces[name] = blocks[:, layer, offset : offset + count].reshape((copies,) + shape)
            offset += count
        layers.append(
            {
                "qkv": jnp.moveaxis(pieces["qkv"], 0, 2).reshape(D, 3, copies * narrow),
                "output": pieces["output"].reshape(copies * narrow, D),
                "up": jnp.moveaxis(pieces["up"], 0, 1).reshape(D, copies * hidden),
                "up_bias": pieces["up_bias"].reshape(copies * hidden),
                "down": pieces["down"].reshape(copies * hidden, D),
            }
        )
    return layers


GROUP = 16
CONV_ROWS = 616
ROOM = 128
HALF = 64
BF16 = jnp.bfloat16
F32 = jnp.float32


def gelu_value(x):
    inner = 0.7978845608028654 * (x + 0.044715 * (x * x * x))
    return 0.5 * x * (1.0 + jnp.tanh(inner))


def gelu_both(x):
    square = x * x
    turn = jnp.tanh(0.7978845608028654 * x * (1.0 + 0.044715 * square))
    half = 0.5 * (1.0 + turn)
    slope = half + 0.5 * x * (1.0 - turn * turn) * (
        0.7978845608028654 * (1.0 + 3 * 0.044715 * square)
    )
    return x * half, slope


def two_parts(x):
    high = x.astype(BF16)
    return high, (x - high.astype(F32)).astype(BF16)


def pair(x):
    return jnp.concatenate(two_parts(x), axis=-1)


def fold_pair(x):
    return x[:, :128] + x[:, 128:]


def dot(a, b):
    return lax.dot_general(a, b, (((1,), (0,)), ((), ())), preferred_element_type=F32)


def dot_rows(a, b):
    return lax.dot_general(a, b, (((0,), (0,)), ((), ())), preferred_element_type=F32)


def lanes():
    return lax.broadcasted_iota(jnp.int32, (1, 128), 1)


def conv_biases(flat_ref):
    lane = lanes()
    one = jnp.where(lane < 32, flat_ref[64:65], 0.0)
    one = one + pltpu.roll(one, 32, 1)
    one = one + pltpu.roll(one, 64, 1)
    two = jnp.where(lane < 64, pltpu.roll(flat_ref[320:321], 96, 1), 0.0)
    two = two + pltpu.roll(two, 64, 1)
    three = jnp.where(
        lane < 32,
        pltpu.roll(flat_ref[608:609], 32, 1),
        jnp.where(lane < 64, pltpu.roll(flat_ref[609:610], 32, 1), 0.0),
    )
    three = three + pltpu.roll(three, 64, 1)
    return one, two, three


def shifted(ref, start, rows, lane):
    first = pltpu.roll(ref[start : start + rows], 128 - lane, 1)
    second = pltpu.roll(ref[start + 1 : start + 1 + rows], 128 - lane, 1)
    return jnp.where(lanes() < 128 - lane, first, second)


def spread_one(flat_ref, put):
    halves = [jnp.transpose(flat_ref[pl.ds(side, 32, stride=2), :]) for side in range(2)]
    turned = jnp.concatenate(halves, axis=0)
    lane = lax.broadcasted_iota(jnp.int32, (8, 128), 1)
    row = lax.broadcasted_iota(jnp.int32, (8, 128), 0)
    low = row < 4
    column = lax.shift_right_logical(lane, 5)
    for ky in range(8):
        for c in range(4):
            held = turned[c * 64 + ky * 8 : c * 64 + ky * 8 + 8]
            wide = jnp.concatenate([held] * 4, axis=1)
            flipped = jnp.concatenate([wide[4:], wide[:4]], axis=0)
            zero = jnp.zeros((8, 128), F32)
            first = jnp.where(column == 0, wide, jnp.where((column == 1) & ~low, flipped, zero))
            second = jnp.where(
                column == 2,
                wide,
                jnp.where(((column == 1) & low) | ((column == 3) & ~low), flipped, zero),
            )
            third = jnp.where((column == 3) & low, flipped, zero)
            put(ky * 128 + c * 32, jnp.concatenate([first, second, third, zero], axis=0))


def spread_two(flat_ref, rows_ref, turned, put):
    lane = lax.broadcasted_iota(jnp.int32, (32, 128), 1)
    rows_ref[0:256] = shifted(flat_ref, 64, 256, 32)
    for j in range(4):
        block = jnp.transpose(rows_ref[pl.ds(j, 64, stride=4), :])
        turned[j * 128 : (j + 1) * 128] = jnp.concatenate([block, block], axis=1)
    for ky in range(4):
        rows = [turned[pl.ds(ky * 4 + kx, 32, stride=16)] for kx in range(4)]
        for i in range(8):
            left = rows[i] if i < 4 else jnp.zeros((32, 128), F32)
            right = rows[i - 2] if 2 <= i < 6 else jnp.zeros((32, 128), F32)
            put(ky * 256 + i * 32, jnp.where(lane < 64, left, right))


def spread_three(flat_ref, rows_ref, turned, put):
    lane = lax.broadcasted_iota(jnp.int32, (64, 128), 1)
    side = lax.broadcasted_iota(jnp.int32, (32, 128), 1) < 64
    rows_ref[0:288] = shifted(flat_ref, 320, 288, 96)
    nine = [rows_ref[pl.ds(k, 32, stride=9), :] for k in range(9)]
    flips = [pltpu.roll(nine[4 + k], 64, 1) for k in range(5)]
    for j in range(5):
        wide = min(128, 576 - j * 128)
        rows_ref[pl.ds(0, 32, stride=2), :] = nine[j]
        rows_ref[pl.ds(1, 32, stride=2), :] = (
            jnp.where(side, flips[j], flips[j + 1]) if j < 4 else flips[4]
        )
        block = jnp.transpose(rows_ref[0:64])[0:wide]
        turned[j * 128 : j * 128 + wide] = jnp.concatenate([block, block], axis=1)
    for ky in range(3):
        rows = [turned[pl.ds(ky * 3 + kx, 64, stride=9)] for kx in range(3)]
        for i in range(4):
            left = rows[i] if i < 3 else jnp.zeros((64, 128), F32)
            right = rows[i - 1] if i >= 1 else jnp.zeros((64, 128), F32)
            put(ky * 256 + i * 64, jnp.where(lane < 64, left, right))


def last_masks():
    return lanes() < 64


def conv_forward_kernel(
    lengths_from,
    frames_ref,
    shared_ref,
    picked_ref,
    z_one_ref,
    z_two_ref,
    z_three_ref,
    flat_ref,
    held,
    wide,
    picked,
    z_one,
    z_two,
    z_three,
    h_one,
    h_two,
    w_one,
    w_two,
    w_three,
    choose,
    rows_ref,
    turned,
    lengths_ref,
    frame_sem,
    out_sem,
):
    scalars = pltpu.make_async_copy(lengths_from, lengths_ref, out_sem.at[5])
    scalars.start()
    scalars.wait()
    wins = lengths_ref.shape[0]
    steps = frames_ref.shape[1]
    used = jnp.int32(0)
    for w in range(wins):
        used = used + lengths_ref[w]
    groups = lax.div(used + (GROUP - 1), GROUP)

    def frame_copy(group, spot, slot):
        state = jnp.minimum(group * GROUP + spot, used - 1)
        window, begin, end = jnp.int32(0), jnp.int32(0), jnp.int32(0)
        for w in range(wins - 1):
            end = end + lengths_ref[w]
            window = jnp.where(state >= end, w + 1, window)
            begin = jnp.where(state >= end, end, begin)
        return pltpu.make_async_copy(
            frames_ref.at[window, state - begin], held.at[slot, spot], frame_sem.at[slot, spot]
        )

    def fetch(group, slot):
        def one(spot, carry):
            frame_copy(group, spot, slot).start()
            return carry

        lax.fori_loop(0, GROUP, one, 0)

    weights = pltpu.make_async_copy(
        shared_ref.at[pl.ds(0, CONV_ROWS)], flat_ref, out_sem.at[4]
    )
    weights.start()
    fetch(0, 0)
    h_one[...] = jnp.zeros(h_one.shape, BF16)

    def put_one(row, block):
        w_one[row : row + 32] = pair(block)

    def put_two(row, block):
        w_two[row : row + 32] = pair(block)

    def put_three(row, block):
        w_three[row : row + 64] = pair(block)

    weights.wait()
    spread_one(flat_ref, put_one)
    spread_two(flat_ref, rows_ref, turned, put_two)
    spread_three(flat_ref, rows_ref, turned, put_three)
    bias_one, bias_two, bias_three = conv_biases(flat_ref)
    row = lax.broadcasted_iota(jnp.int32, (128, 640), 0)
    column = lax.broadcasted_iota(jnp.int32, (128, 640), 1)
    place = jnp.bitwise_and(column, 31)
    channel = jnp.bitwise_and(lax.shift_right_logical(column, 5), 3)
    block = lax.shift_right_logical(column, 7)
    right = (row == 16 * block + place) & (place < 20)
    for c in range(4):
        choose[c * 128 : (c + 1) * 128] = jnp.where(right & (channel == c), 1.0, 0.0).astype(BF16)

    def one_group(group, carry):
        slot = lax.rem(group, 2)

        @pl.when(group + 1 < groups)
        def ahead():
            fetch(group + 1, 1 - slot)

        def lay(step, carry):
            spots = [step * 4 + k for k in range(4)]
            for spot in spots:
                frame_copy(group, spot, slot).wait()
            for spot in spots:
                image = held[slot, spot].astype(F32).reshape(336, 84)
                image = jnp.concatenate([image, jnp.zeros((336, 44), F32)], axis=1)
                wide[pl.ds(spot, 336, stride=GROUP), :] = image
            return carry

        lax.fori_loop(0, GROUP // 4, lay, 0)
        for part in range(3):
            rows = wide[part * 1792 : (part + 1) * 1792].reshape(28, 4, GROUP, 128)
            rows = [rows[:, c].reshape(448, 128).astype(BF16) for c in range(4)]
            result = dot(jnp.concatenate(rows, axis=1), choose[...])
            picked[part * 7 : (part + 1) * 7] = result.astype(BF16).reshape(7, 4, GROUP, 640)
        keep_picked = pltpu.make_async_copy(picked, picked_ref.at[group], out_sem.at[0])
        keep_picked.start()
        for q in range(5):
            pieces = [
                picked[j : j + 20, b, :, q * 128 : (q + 1) * 128].reshape(20 * GROUP, 128)
                for j in range(2)
                for b in range(4)
            ]
            z = fold_pair(dot(jnp.concatenate(pieces, axis=1), w_one[...])) + bias_one
            z_one[:, :, q] = z.reshape(10, 2, GROUP, 128)
            high, low = two_parts(gelu_value(z))
            h_one[0, :, :, q] = high.reshape(10, 2, GROUP, 128)
            h_one[1, :, :, q] = low.reshape(10, 2, GROUP, 128)
        keep_one = pltpu.make_async_copy(z_one, z_one_ref.at[group], out_sem.at[1])
        keep_one.start()
        total = jnp.zeros((45 * GROUP, 128), F32)
        for part in range(2):
            pieces = []
            for j in range(2):
                for b in range(2):
                    pieces.append(h_one[part, j : j + 9, b, 0:5].reshape(45 * GROUP, 128))
                    pieces.append(h_one[part, j : j + 9, b, 1:6].reshape(45 * GROUP, 128))
            total = total + fold_pair(dot(jnp.concatenate(pieces, axis=1), w_two[...]))
        z = (total + bias_two).reshape(9, 5, GROUP, 128)
        z_two[...] = z
        h = gelu_value(z)
        high, low = two_parts(h)
        h_two[0] = high
        h_two[1] = low
        edge = jnp.where(last_masks(), h[:, 4].reshape(9 * GROUP, 128), 0.0)
        high, low = two_parts(edge)
        h_two[0, :, 4] = high.reshape(9, GROUP, 128)
        h_two[1, :, 4] = low.reshape(9, GROUP, 128)
        keep_two = pltpu.make_async_copy(z_two, z_two_ref.at[group], out_sem.at[2])
        keep_two.start()
        total = jnp.zeros((28 * GROUP, 128), F32)
        for part in range(2):
            pieces = []
            for ky in range(3):
                pieces.append(h_two[part, ky : ky + 7, 0:4].reshape(28 * GROUP, 128))
                pieces.append(h_two[part, ky : ky + 7, 1:5].reshape(28 * GROUP, 128))
            total = total + fold_pair(dot(jnp.concatenate(pieces, axis=1), w_three[...]))
        z_three[...] = (total + bias_three).reshape(28, GROUP, 128)
        spot = pl.multiple_of(group * GROUP, GROUP)
        keep_three = pltpu.make_async_copy(
            z_three, z_three_ref.at[:, pl.ds(spot, GROUP)], out_sem.at[3]
        )
        keep_three.start()
        keep_picked.wait()
        keep_one.wait()
        keep_two.wait()
        keep_three.wait()
        return carry

    lax.fori_loop(0, groups, one_group, 0)


def conv_forward(lengths, frames, flat):
    most = ROOM // GROUP
    any_spec = pl.BlockSpec(memory_space=pl.ANY)
    hbm = pl.BlockSpec(memory_space=pltpu.HBM)
    return pl.pallas_call(
        conv_forward_kernel,
        in_specs=[
            any_spec,
            any_spec,
            any_spec,
        ],
        out_specs=[hbm] * 4,
        out_shape=[
            jax.ShapeDtypeStruct((most, 21, 4, GROUP, 640), BF16),
            jax.ShapeDtypeStruct((most, 10, 2, 5, GROUP, 128), F32),
            jax.ShapeDtypeStruct((most, 9, 5, GROUP, 128), F32),
            jax.ShapeDtypeStruct((28, ROOM, 128), F32),
        ],
        scratch_shapes=[
            pltpu.VMEM((CONV_ROWS, 128), F32),
            pltpu.VMEM((2, GROUP, 84, 4, 84), BF16),
            pltpu.VMEM((336 * GROUP, 128), F32),
            pltpu.VMEM((21, 4, GROUP, 640), BF16),
            pltpu.VMEM((10, 2, 5, GROUP, 128), F32),
            pltpu.VMEM((9, 5, GROUP, 128), F32),
            pltpu.VMEM((28, GROUP, 128), F32),
            pltpu.VMEM((2, 10, 2, 6, GROUP, 128), BF16),
            pltpu.VMEM((2, 9, 5, GROUP, 128), BF16),
            pltpu.VMEM((1024, 256), BF16),
            pltpu.VMEM((1024, 256), BF16),
            pltpu.VMEM((768, 256), BF16),
            pltpu.VMEM((512, 640), BF16),
            pltpu.VMEM((288, 128), F32),
            pltpu.VMEM((576, 128), F32),
            pltpu.SMEM(lengths.shape, jnp.int32),
            pltpu.SemaphoreType.DMA((2, GROUP)),
            pltpu.SemaphoreType.DMA((6,)),
        ],
        compiler_params=pltpu.CompilerParams(vmem_limit_bytes=62 * 1024 * 1024),
        name="conv_forward",
    )(lengths, frames.transpose(0, 1, 3, 2, 4), flat)


def gather_one(total, out):
    lane = lax.broadcasted_iota(jnp.int32, (32, 128), 1)
    halves = [jnp.zeros((32, 128), F32) for side in range(2)]
    for ky in range(8):
        held = total[0:128, ky * 128 : (ky + 1) * 128] + total[128:256, ky * 128 : (ky + 1) * 128]
        summed = held[0:32]
        for o in range(1, 4):
            summed = summed + pltpu.roll(held[32 * o : 32 * o + 32], 128 - 4 * o, 1)
        for c in range(4):
            spot = (c % 2) * 64 + ky * 8
            shift = (spot - c * 32) % 128
            moved = pltpu.roll(summed, shift, 1) if shift else summed
            inside = (lane >= spot) & (lane < spot + 8)
            halves[c // 2] = halves[c // 2] + jnp.where(inside, moved, 0.0)
    for side in range(2):
        out[pl.ds(side, 32, stride=2), :] = halves[side]


def gather_two(total, turned, rows_ref, out):
    lane = lax.broadcasted_iota(jnp.int32, (64, 128), 1)
    for ky in range(4):
        near = total[0:128, ky * 256 : ky * 256 + 128] + total[128:256, ky * 256 : ky * 256 + 128]
        far = (
            total[0:128, ky * 256 + 128 : ky * 256 + 256]
            + total[128:256, ky * 256 + 128 : ky * 256 + 256]
        )
        summed = near[0:64] + jnp.where(
            lane < 64, pltpu.roll(near[64:128], 64, 1), pltpu.roll(far[64:128], 64, 1)
        )
        flipped = jnp.transpose(jnp.concatenate([summed, jnp.zeros((64, 128), F32)], axis=0))
        for kx in range(4):
            turned[pl.ds(ky * 4 + kx, 32, stride=16), :] = flipped[kx * 32 : (kx + 1) * 32]
    rows_ref[0:8] = jnp.zeros((8, 128), F32)
    rows_ref[264:272] = jnp.zeros((8, 128), F32)
    for j in range(4):
        block = jnp.transpose(turned[j * 128 : (j + 1) * 128])[0:64]
        rows_ref[pl.ds(8 + j, 64, stride=4), :] = block
    own = pltpu.roll(rows_ref[8:265], 32, 1)
    before = pltpu.roll(rows_ref[7:264], 32, 1)
    out[64:321] = jnp.where(lanes() >= 32, own, before)


def gather_three(total, turned, rows_ref, out):
    lane = lax.broadcasted_iota(jnp.int32, (64, 128), 1)
    side = lax.broadcasted_iota(jnp.int32, (32, 128), 1) < 64
    blank = jnp.zeros((64, 128), F32)
    for ky in range(3):
        near = total[0:128, ky * 256 : ky * 256 + 128] + total[128:256, ky * 256 : ky * 256 + 128]
        far = (
            total[0:128, ky * 256 + 128 : ky * 256 + 256]
            + total[128:256, ky * 256 + 128 : ky * 256 + 256]
        )
        first = near[0:64] + jnp.where(
            lane < 64, pltpu.roll(near[64:128], 64, 1), pltpu.roll(far[64:128], 64, 1)
        )
        second = far[0:64] + pltpu.roll(far[64:128], 64, 1)
        flipped = jnp.transpose(jnp.concatenate([first, blank], axis=0))
        turned[pl.ds(ky * 3, 64, stride=9), :] = flipped[0:64]
        turned[pl.ds(ky * 3 + 1, 64, stride=9), :] = flipped[64:128]
        flipped = jnp.transpose(jnp.concatenate([second, blank], axis=0))
        turned[pl.ds(ky * 3 + 2, 64, stride=9), :] = flipped[0:64]
    turned[576:640] = blank
    evens, odds = [], []
    for j in range(5):
        rows_ref[0:64] = jnp.transpose(turned[j * 128 : (j + 1) * 128])[0:64]
        evens.append(rows_ref[pl.ds(0, 32, stride=2), :])
        odds.append(pltpu.roll(rows_ref[pl.ds(1, 32, stride=2), :], 64, 1))
    rows_ref[0:8] = jnp.zeros((8, 128), F32)
    rows_ref[296:304] = jnp.zeros((8, 128), F32)
    for k in range(9):
        if k < 4:
            held = evens[k]
        elif k == 4:
            held = jnp.where(side, evens[4], odds[0])
        else:
            held = jnp.where(side, odds[k - 5], odds[k - 4])
        rows_ref[pl.ds(8 + k, 32, stride=9), :] = held
    own = pltpu.roll(rows_ref[8:297], 96, 1)
    before = pltpu.roll(rows_ref[7:296], 96, 1)
    edge = out[320:321]
    out[320:609] = jnp.where(lanes() >= 96, own, before)
    out[320:321] = out[320:321] + edge


def conv_backward_kernel(
    lengths_from,
    picked_ref,
    z_one_ref,
    z_two_ref,
    d_three_ref,
    shared_ref,
    flat_out,
    flat_ref,
    picked,
    z_one,
    z_two,
    d_three,
    h_one,
    h_two,
    slope_one,
    pad_three,
    pad_two,
    d_one,
    v_two,
    v_three,
    spread,
    rows_ref,
    turned,
    bias_out,
    total_one,
    total_two,
    total_three,
    lengths_ref,
    load_sem,
    weight_sem,
):
    scalars = pltpu.make_async_copy(lengths_from, lengths_ref, weight_sem)
    scalars.start()
    scalars.wait()
    used = jnp.int32(0)
    for w in range(lengths_ref.shape[0]):
        used = used + lengths_ref[w]
    groups = lax.div(used + (GROUP - 1), GROUP)

    def loads(group, slot):
        spot = pl.multiple_of(group * GROUP, GROUP)
        return [
            pltpu.make_async_copy(picked_ref.at[group], picked.at[slot], load_sem.at[slot, 0]),
            pltpu.make_async_copy(z_one_ref.at[group], z_one.at[slot], load_sem.at[slot, 1]),
            pltpu.make_async_copy(z_two_ref.at[group], z_two.at[slot], load_sem.at[slot, 2]),
            pltpu.make_async_copy(
                d_three_ref.at[:, pl.ds(spot, GROUP)], d_three.at[slot], load_sem.at[slot, 3]
            ),
        ]

    weights = pltpu.make_async_copy(
        shared_ref.at[pl.ds(0, CONV_ROWS)], flat_ref, weight_sem
    )
    weights.start()
    for load in loads(0, 0):
        load.start()

    def put_two(row, block):
        spread[row : row + 32] = block

    def put_three(row, block):
        spread[row : row + 64] = block

    weights.wait()
    spread_two(flat_ref, rows_ref, turned, put_two)
    for b in range(2):
        for j in range(2):
            for side in range(2):
                source = (2 * j + b) * 256 + side * 128
                target = (b * 2 + j) * 256 + side * 128
                v_two[target : target + 128] = pair(jnp.transpose(spread[source : source + 128]))
    spread_three(flat_ref, rows_ref, turned, put_three)
    for part in range(6):
        rows = pl.ds(part * 128, 128)
        v_three[rows] = pair(jnp.transpose(spread[rows]))
    total_one[...] = jnp.zeros(total_one.shape, F32)
    total_two[...] = jnp.zeros(total_two.shape, F32)
    total_three[...] = jnp.zeros(total_three.shape, F32)
    bias_out[...] = jnp.zeros(bias_out.shape, F32)
    h_one[...] = jnp.zeros(h_one.shape, BF16)
    pad_two[...] = jnp.zeros(pad_two.shape, BF16)
    pad_three[...] = jnp.zeros(pad_three.shape, BF16)

    def fold(rows):
        return jnp.sum(rows.reshape(-1, 8, 128), axis=0)

    def one_group(group, carry):
        slot = lax.rem(group, 2)

        @pl.when(group + 1 < groups)
        def ahead():
            for load in loads(group + 1, 1 - slot):
                load.start()

        for load in loads(group, slot):
            load.wait()
        rows = d_three[slot].reshape(28 * GROUP, 128)
        bias_out[2] += fold(rows)
        both = pair(rows)
        pad_three[0, 2:9, 1:5] = both[:, :128].reshape(7, 4, GROUP, 128)
        pad_three[1, 2:9, 1:5] = both[:, 128:].reshape(7, 4, GROUP, 128)
        h, slope_two = gelu_both(z_two[slot])
        high, low = two_parts(h)
        h_two[0] = high
        h_two[1] = low
        edge = jnp.where(last_masks(), h[:, 4].reshape(9 * GROUP, 128), 0.0)
        high, low = two_parts(edge)
        h_two[0, :, 4] = high.reshape(9, GROUP, 128)
        h_two[1, :, 4] = low.reshape(9, GROUP, 128)
        for part in range(2):
            pieces = []
            for ky in range(3):
                pieces.append(h_two[part, ky : ky + 7, 0:4].reshape(28 * GROUP, 128))
                pieces.append(h_two[part, ky : ky + 7, 1:5].reshape(28 * GROUP, 128))
            total_three[...] += dot_rows(both, jnp.concatenate(pieces, axis=1))
        spill = jnp.zeros((45 * GROUP, 128), F32)
        for part in range(2):
            pieces = []
            for ky in range(3):
                pieces.append(pad_three[part, 2 - ky : 11 - ky, 1:6].reshape(45 * GROUP, 128))
                pieces.append(pad_three[part, 2 - ky : 11 - ky, 0:5].reshape(45 * GROUP, 128))
            spill = spill + fold_pair(dot(jnp.concatenate(pieces, axis=1), v_three[...]))
        rows = spill * slope_two.reshape(45 * GROUP, 128)
        bias_out[1] += fold(rows)
        both = pair(rows)
        pad_two[0, 1:10, 1:6] = both[:, :128].reshape(9, 5, GROUP, 128)
        pad_two[1, 1:10, 1:6] = both[:, 128:].reshape(9, 5, GROUP, 128)
        for q in range(5):
            h, slope = gelu_both(z_one[slot, :, :, q])
            high, low = two_parts(h)
            h_one[0, :, :, q] = high
            h_one[1, :, :, q] = low
            slope_one[:, :, q] = slope
        for part in range(2):
            pieces = []
            for j in range(2):
                for b in range(2):
                    pieces.append(h_one[part, j : j + 9, b, 0:5].reshape(45 * GROUP, 128))
                    pieces.append(h_one[part, j : j + 9, b, 1:6].reshape(45 * GROUP, 128))
            total_two[...] += dot_rows(both, jnp.concatenate(pieces, axis=1))
        for b in range(2):
            spill = jnp.zeros((50 * GROUP, 128), F32)
            for part in range(2):
                pieces = []
                for j in range(2):
                    pieces.append(pad_two[part, 1 - j : 11 - j, 1:6].reshape(50 * GROUP, 128))
                    pieces.append(pad_two[part, 1 - j : 11 - j, 0:5].reshape(50 * GROUP, 128))
                spill = spill + fold_pair(
                    dot(jnp.concatenate(pieces, axis=1), v_two[b * 512 : (b + 1) * 512])
                )
            rows = spill * slope_one[:, b].reshape(50 * GROUP, 128)
            bias_out[0] += fold(rows)
            d_one[:, b] = pair(rows).reshape(10, 5, GROUP, 256)
        for q in range(5):
            pieces = [
                picked[slot, j : j + 20, b, :, q * 128 : (q + 1) * 128].reshape(20 * GROUP, 128)
                for j in range(2)
                for b in range(4)
            ]
            total_one[...] += dot_rows(
                d_one[:, :, q].reshape(20 * GROUP, 256), jnp.concatenate(pieces, axis=1)
            )
        return carry

    lax.fori_loop(0, groups, one_group, 0)
    gather_one(total_one, flat_out)
    gather_two(total_two, turned, rows_ref, flat_out)
    gather_three(total_three, turned, rows_ref, flat_out)
    lane = lanes()
    sums = [jnp.sum(bias_out[k], axis=0, keepdims=True) for k in range(3)]
    sums[0] = sums[0] + pltpu.roll(sums[0], 64, 1)
    sums[0] = sums[0] + pltpu.roll(sums[0], 32, 1)
    sums[1] = jnp.where(lane < 64, sums[1] + pltpu.roll(sums[1], 64, 1), 0.0)
    sums[2] = jnp.where(lane < 64, sums[2] + pltpu.roll(sums[2], 64, 1), 0.0)
    flat_out[64:65] = jnp.where(lane < 32, sums[0], flat_out[64:65])
    flat_out[320:321] = flat_out[320:321] + pltpu.roll(sums[1], 32, 1)
    late = pltpu.roll(sums[2], 96, 1)
    flat_out[608:609] = flat_out[608:609] + jnp.where(lane >= 96, late, 0.0)
    row = lax.broadcasted_iota(jnp.int32, (7, 128), 0)
    flat_out[609:616] = jnp.where((row == 0) & (lane < 32), late, 0.0)


def conv_backward(lengths, picked, z_one, z_two, d_three, flat):
    hbm = pl.BlockSpec(memory_space=pltpu.HBM)
    vmem = pl.BlockSpec(memory_space=pltpu.VMEM)
    return pl.pallas_call(
        conv_backward_kernel,
        in_specs=[hbm] * 6,
        out_specs=vmem,
        out_shape=jax.ShapeDtypeStruct((CONV_ROWS, 128), F32),
        scratch_shapes=[
            pltpu.VMEM((CONV_ROWS, 128), F32),
            pltpu.VMEM((2, 21, 4, GROUP, 640), BF16),
            pltpu.VMEM((2, 10, 2, 5, GROUP, 128), F32),
            pltpu.VMEM((2, 9, 5, GROUP, 128), F32),
            pltpu.VMEM((2, 28, GROUP, 128), F32),
            pltpu.VMEM((2, 10, 2, 6, GROUP, 128), BF16),
            pltpu.VMEM((2, 9, 5, GROUP, 128), BF16),
            pltpu.VMEM((10, 2, 5, GROUP, 128), F32),
            pltpu.VMEM((2, 11, 6, GROUP, 128), BF16),
            pltpu.VMEM((2, 11, 6, GROUP, 128), BF16),
            pltpu.VMEM((10, 2, 5, GROUP, 256), BF16),
            pltpu.VMEM((1024, 256), BF16),
            pltpu.VMEM((768, 256), BF16),
            pltpu.VMEM((1024, 128), F32),
            pltpu.VMEM((304, 128), F32),
            pltpu.VMEM((640, 128), F32),
            pltpu.VMEM((3, 8, 128), F32),
            pltpu.VMEM((256, 1024), F32),
            pltpu.VMEM((256, 1024), F32),
            pltpu.VMEM((256, 768), F32),
            pltpu.SMEM(lengths.shape, jnp.int32),
            pltpu.SemaphoreType.DMA((2, 4)),
            pltpu.SemaphoreType.DMA,
        ],
        compiler_params=pltpu.CompilerParams(vmem_limit_bytes=62 * 1024 * 1024),
        name="conv_backward",
    )(lengths, picked, z_one, z_two, d_three, flat)


HIGH = lax.Precision.HIGH
VECTORS_ROW = 3745
TIME_ROW = 3780


def mm(a, b):
    return lax.dot_general(
        a, b, (((1,), (0,)), ((), ())), precision=HIGH, preferred_element_type=F32
    )


def mm_nt(a, b):
    return lax.dot_general(
        a, b, (((1,), (1,)), ((), ())), precision=HIGH, preferred_element_type=F32
    )


def mm_tn(a, b):
    return lax.dot_general(
        a, b, (((0,), (0,)), ((), ())), precision=HIGH, preferred_element_type=F32
    )


def dot_nt(a, b):
    return lax.dot_general(a, b, (((1,), (1,)), ((), ())), preferred_element_type=F32)


def norm_parts(stream):
    centered = stream - jnp.mean(stream, -1, keepdims=True)
    spread = jnp.mean(centered * centered, -1, keepdims=True)
    scale = lax.rsqrt(spread + 1e-05)
    return centered * scale, scale


def norm_back(grad, unit, scale, gain):
    grad = grad * gain
    inner = jnp.mean(grad * unit, -1, keepdims=True)
    return scale * (grad - jnp.mean(grad, -1, keepdims=True) - unit * inner)


def column_sum(x):
    return jnp.sum(x, axis=0, keepdims=True)


def head_places():
    number = lax.broadcasted_iota(jnp.int32, (128, 128), 0) * ACT
    lane = lax.broadcasted_iota(jnp.int32, (128, 128), 1)
    row = lax.shift_right_logical(number, 7)
    return row + jnp.where(lane < jnp.bitwise_and(number, 127), 1, 0)


def roll_rows(held, sign):
    number = lax.broadcasted_iota(jnp.int32, (128, 128), 0) * ACT
    for k in range(7):
        moved = pltpu.roll(held, (sign * (1 << k)) % 128, 1)
        held = jnp.where(jnp.bitwise_and(number, 1 << k) > 0, moved, held)
    return held


def square_head(rows):
    place = head_places()
    held = jnp.zeros((128, 128), F32)
    for k in range(ACT):
        held = jnp.where(place == k, rows[k : k + 1], held)
    held = roll_rows(held, -1)
    lane = lax.broadcasted_iota(jnp.int32, (128, 128), 1)
    return jnp.where(lane < ACT, held, 0.0)


def flat_head(grads):
    place = head_places()
    lane = lax.broadcasted_iota(jnp.int32, (128, 128), 1)
    held = roll_rows(jnp.where(lane < ACT, grads, 0.0), 1)
    rows = [
        jnp.sum(jnp.where(place == k, held, 0.0), axis=0, keepdims=True) for k in range(ACT)
    ]
    return jnp.concatenate(rows + [jnp.zeros((24 - ACT, 128), F32)], axis=0)


def unpack_split(split_ref, qkv, output, up, up_bias, down):
    lane = lax.broadcasted_iota(jnp.int32, (32, 128), 1)
    for layer in range(LAYERS):
        base = layer * 385
        kinds = [[jnp.zeros((32, 128), F32) for j in range(4)] for kind in range(3)]
        for m in range(4):
            rows = [split_ref[m, pl.ds(base + k, 32, stride=3), :] for k in range(3)]
            inside = (lane >= 32 * m) & (lane < 32 * m + 32)
            for j in range(4):
                for kind in range(3):
                    spot = j * 96 + kind * 32
                    source = rows[spot // 128]
                    shift = (32 * m - spot % 128) % 128
                    moved = pltpu.roll(source, shift, 1) if shift else source
                    kinds[kind][j] = jnp.where(inside, moved, kinds[kind][j])
            output[layer, 32 * m : 32 * m + 32] = split_ref[m, base + 96 : base + 128]
            up[layer, :, 128 * m : 128 * m + 128] = split_ref[m, base + 128 : base + 256]
            up_bias[layer, :, 128 * m : 128 * m + 128] = split_ref[m, base + 256 : base + 257]
            down[layer, 128 * m : 128 * m + 128] = split_ref[m, base + 257 : base + 385]
        for kind in range(3):
            for j in range(4):
                qkv[layer, kind, pl.ds(j, 32, stride=4), :] = kinds[kind][j]


def pack_split(out_ref, qkv, output, up, up_bias, down):
    lane = lax.broadcasted_iota(jnp.int32, (32, 128), 1)
    for layer in range(LAYERS):
        base = layer * 385
        parts = [[qkv[layer, kind, pl.ds(j, 32, stride=4), :] for j in range(4)] for kind in range(3)]
        for m in range(4):
            rows = [jnp.zeros((32, 128), F32) for k in range(3)]
            for j in range(4):
                for kind in range(3):
                    spot = j * 96 + kind * 32
                    low = spot % 128
                    shift = (low - 32 * m) % 128
                    moved = pltpu.roll(parts[kind][j], shift, 1) if shift else parts[kind][j]
                    inside = (lane >= low) & (lane < low + 32)
                    rows[spot // 128] = jnp.where(inside, moved, rows[spot // 128])
            for k in range(3):
                out_ref[m, pl.ds(base + k, 32, stride=3), :] = rows[k]
            out_ref[m, base + 96 : base + 128] = output[layer, 32 * m : 32 * m + 32]
            out_ref[m, base + 128 : base + 256] = up[layer, :, 128 * m : 128 * m + 128]
            out_ref[m, base + 256 : base + 257] = up_bias[layer, :, 128 * m : 128 * m + 128]
            out_ref[m, base + 257 : base + 385] = down[layer, 128 * m : 128 * m + 128]
    for m in range(4):
        out_ref[m, 770:784] = jnp.zeros((14, 128), F32)


def former_body(
    slots,
    used,
    lengths_ref,
    returns_ref,
    actions_ref,
    head_ref,
    z_ref,
    small,
    times_all,
    encoder,
    weights,
    d_three_ref,
    d_encoder_ref,
    d_small_ref,
    d_times_ref,
    grads,
    chances,
    kept,
    sums,
    flats,
):
    qkv, output, up, up_bias, down = weights
    d_qkv, d_output, d_up, d_up_bias, d_down = grads
    rows = 3 * slots
    wins, steps = returns_ref.shape
    vec = [small[k : k + 1] for k in range(17)]
    table = small[17 : 17 + ACT]
    slot = lax.broadcasted_iota(jnp.int32, (slots, 1), 0)
    window = jnp.zeros((slots, 1), jnp.int32)
    begin = jnp.zeros((slots, 1), jnp.int32)
    end = jnp.int32(0)
    for w in range(wins - 1):
        end = end + lengths_ref[w]
        window = jnp.where(slot >= end, w + 1, window)
        begin = jnp.where(slot >= end, end, begin)
    moment = slot - begin
    valid = slot < used
    time_lane = lax.broadcasted_iota(jnp.int32, (slots, steps), 1)
    amount = jnp.zeros((slots, 1), F32)
    action = jnp.zeros((slots, 1), jnp.int32)
    for w in range(wins):
        here = (time_lane == moment) & (window == w)
        amount = amount + jnp.sum(
            jnp.where(here, returns_ref[w : w + 1], 0.0), axis=1, keepdims=True
        )
        action = action + jnp.sum(jnp.where(here, actions_ref[w : w + 1], 0), axis=1, keepdims=True)
    lane = lax.broadcasted_iota(jnp.int32, (slots, 128), 1)
    picks = jnp.where((lane == action) & valid, 1.0, 0.0)
    reward = jnp.tanh(amount * vec[14] + vec[15])
    table = jnp.concatenate([table, jnp.zeros((128 - ACT, 128), F32)], axis=0)
    move = jnp.tanh(mm(picks, table))
    sum_state = jnp.zeros((slots, 128), F32)
    for k in range(28):
        z = jnp.where(valid, z_ref[k, 0:slots], 0.0)
        high, low = two_parts(gelu_value(z))
        flats[0, 0:slots, k * 128 : (k + 1) * 128] = high
        flats[1, 0:slots, k * 128 : (k + 1) * 128] = low
    for part in range(2):
        sum_state = sum_state + fold_pair(dot(flats[part, 0:slots], encoder[...]))
    state = jnp.tanh(sum_state + vec[16])
    times = times_all[0:slots]
    stream = jnp.concatenate([reward + times, state + times, move + times], axis=0)

    def ids(axis):
        shape = (rows, 1) if axis == 0 else (1, rows)
        number = lax.broadcasted_iota(jnp.int32, shape, axis)
        kind = jnp.where(number >= 2 * slots, 2, jnp.where(number >= slots, 1, 0))
        return number - kind * slots, kind

    (slot_q, kind_q), (slot_k, kind_k) = ids(0), ids(1)

    def begin_of(slot_ids):
        found = jnp.zeros(slot_ids.shape, jnp.int32)
        end = jnp.int32(0)
        for w in range(wins - 1):
            end = end + lengths_ref[w]
            found = jnp.where(slot_ids >= end, end, found)
        return found

    order_q = slot_q * 3 + kind_q
    order_k = slot_k * 3 + kind_k
    allowed = (order_q >= order_k) & (slot_k >= begin_of(slot_q)) & (slot_k < used)
    head_of = lax.shift_right_logical(lax.broadcasted_iota(jnp.int32, (1, 128), 1), 4)
    heads = D // HD
    batch = 4 if slots <= HALF else 2

    def masked(x, masks):
        return jnp.concatenate([jnp.where(mask, x, jnp.zeros_like(x)) for mask in masks], axis=0)

    def unmasked(x, masks):
        held = jnp.where(masks[0], x[0:rows], 0.0)
        for k in range(1, batch):
            held = held + jnp.where(masks[k], x[k * rows : (k + 1) * rows], 0.0)
        return held

    tape = []
    for layer in range(LAYERS):
        gains = vec[6 * layer : 6 * layer + 6]
        unit_one, scale_one = norm_parts(stream)
        normed = unit_one * gains[0] + gains[1]
        wide = jnp.concatenate([qkv[layer, k] for k in range(3)], axis=1)
        mixed = mm(normed, wide)
        query_high, query_low = two_parts(mixed[:, :128] * 0.25)
        keys, values = pair(mixed[:, 128:256]), pair(mixed[:, 256:])
        kept[layer, 0, 0:rows] = query_high
        kept[layer, 1, 0:rows] = query_low
        for k in range(2):
            kept[layer, 2 + k, 0:rows] = keys[:, k * 128 : (k + 1) * 128]
            kept[layer, 4 + k, 0:rows] = values[:, k * 128 : (k + 1) * 128]
        sums[0, 0:rows] = jnp.zeros((rows, 128), F32)

        def attend(turn, carry, layer=layer):
            masks = [head_of == turn * batch + k for k in range(batch)]
            parts = [masked(kept[layer, k, 0:rows], masks) for k in range(2)]
            keys = [kept[layer, 2 + k, 0:rows] for k in range(2)]
            values = [kept[layer, 4 + k, 0:rows] for k in range(2)]
            scores = dot_nt(
                jnp.concatenate([parts[0], parts[0]], axis=1), jnp.concatenate(keys, axis=1)
            )
            scores = (scores + dot_nt(parts[1], keys[0])).reshape(batch, rows, rows)
            scores = jnp.where(allowed[None], scores, -1e30)
            peak = jnp.max(scores, -1, keepdims=True)
            chance = jnp.exp(scores - peak)
            chance = chance / jnp.sum(chance, -1, keepdims=True)
            high, low = two_parts(chance.reshape(batch * rows, rows))
            spot = pl.ds(pl.multiple_of(turn * (batch * rows), 64), batch * rows)
            chances[layer, 0, spot, 0:rows] = high
            chances[layer, 1, spot, 0:rows] = low
            seen = fold_pair(dot(high, jnp.concatenate(values, axis=1))) + dot(low, values[0])
            sums[0, 0:rows] += unmasked(seen, masks)
            return carry

        lax.fori_loop(0, heads // batch, attend, 0)
        context = sums[0, 0:rows]
        stream = stream + mm(context, output[layer]) + gains[4]
        unit_two, scale_two = norm_parts(stream)
        normed_two = unit_two * gains[2] + gains[3]
        inner, slope = gelu_both(mm(normed_two, up[layer]) + up_bias[layer])
        stream = stream + mm(inner, down[layer]) + gains[5]
        tape.append((unit_one, scale_one, unit_two, scale_two, inner, slope, context))
    end_stream = stream[slots : 2 * slots]
    unit, scale = norm_parts(end_stream)
    final = unit * vec[12] + vec[13]
    logits = jnp.where(lane < ACT, mm(final, head_ref[...]), -1e30)
    peak = jnp.max(logits, -1, keepdims=True)
    powers = jnp.exp(logits - peak)
    total = jnp.sum(powers, -1, keepdims=True)
    chosen = jnp.sum(jnp.where(lane == action, logits, 0.0), -1, keepdims=True)
    terms = jnp.where(valid, jnp.log(total) + peak - chosen, 0.0)
    loss = jnp.sum(terms, axis=0, keepdims=True)
    d_small_ref[72:80] = jnp.broadcast_to(loss, (8, 128))
    d_logits = jnp.where(valid, powers / total, 0.0) - picks
    d_small_ref[48:72] = flat_head(mm_tn(final, d_logits))
    d_final = mm_nt(d_logits, head_ref[...])
    d_vec = [None] * 17
    d_vec[12] = column_sum(d_final * unit)
    d_vec[13] = column_sum(d_final)
    d_end = norm_back(d_final, unit, scale, vec[12])
    blank = jnp.zeros((slots, 128), F32)
    d_stream = jnp.concatenate([blank, d_end, blank], axis=0)
    for layer in reversed(range(LAYERS)):
        unit_one, scale_one, unit_two, scale_two, inner, slope, context = tape[layer]
        gains = vec[6 * layer : 6 * layer + 6]
        d_vec[6 * layer + 5] = column_sum(d_stream)
        d_down[layer] = mm_tn(inner, d_stream)
        d_inner = mm_nt(d_stream, down[layer]) * slope
        d_up_bias[layer] = column_sum(d_inner)
        normed_two = unit_two * gains[2] + gains[3]
        d_up[layer] = mm_tn(normed_two, d_inner)
        d_normed = mm_nt(d_inner, up[layer])
        d_vec[6 * layer + 2] = column_sum(d_normed * unit_two)
        d_vec[6 * layer + 3] = column_sum(d_normed)
        d_stream = d_stream + norm_back(d_normed, unit_two, scale_two, gains[2])
        d_vec[6 * layer + 4] = column_sum(d_stream)
        d_output[layer] = mm_tn(context, d_stream)
        d_context = mm_nt(d_stream, output[layer])
        bases = d_context * context
        high, low = two_parts(d_context)
        for k in range(3):
            sums[k, 0:rows] = jnp.zeros((rows, 128), F32)
        kept[layer, 6, 0:rows] = high
        kept[layer, 7, 0:rows] = low
        sums[3, 0:rows] = bases

        def attend_back(turn, carry, layer=layer):
            masks = [head_of == turn * batch + k for k in range(batch)]
            query = [masked(kept[layer, k, 0:rows], masks) for k in range(2)]
            keys = [kept[layer, 2 + k, 0:rows] for k in range(2)]
            values = [kept[layer, 4 + k, 0:rows] for k in range(2)]
            d_seen = [masked(kept[layer, 6 + k, 0:rows], masks) for k in range(2)]
            base = jnp.sum(masked(sums[3, 0:rows], masks), -1, keepdims=True)
            spot = pl.ds(pl.multiple_of(turn * (batch * rows), 64), batch * rows)
            chance = [chances[layer, k, spot, 0:rows] for k in range(2)]
            d_chance = dot_nt(
                jnp.concatenate([d_seen[0], d_seen[0]], axis=1), jnp.concatenate(values, axis=1)
            )
            d_chance = d_chance + dot_nt(d_seen[1], values[0])
            d_scores = (chance[0].astype(F32) + chance[1].astype(F32)) * (d_chance - base)
            high, low = two_parts(d_scores)
            d_query = fold_pair(dot(high, jnp.concatenate(keys, axis=1))) + dot(low, keys[0])
            sums[0, 0:rows] += unmasked(d_query, masks)
            d_keys = fold_pair(dot_rows(high, jnp.concatenate(query, axis=1)))
            sums[1, 0:rows] += d_keys + dot_rows(low, query[0])
            d_values = fold_pair(dot_rows(chance[0], jnp.concatenate(d_seen, axis=1)))
            sums[2, 0:rows] += d_values + dot_rows(chance[1], d_seen[0])
            return carry

        lax.fori_loop(0, heads // batch, attend_back, 0)
        normed = unit_one * gains[0] + gains[1]
        d_mixed = jnp.concatenate(
            [sums[0, 0:rows] * 0.25, sums[1, 0:rows], sums[2, 0:rows]], axis=1
        )
        wide = jnp.concatenate([qkv[layer, k] for k in range(3)], axis=1)
        d_wide = mm_tn(normed, d_mixed)
        for k in range(3):
            d_qkv[layer, k] = d_wide[:, k * 128 : (k + 1) * 128]
        d_normed = mm_nt(d_mixed, wide)
        d_vec[6 * layer] = column_sum(d_normed * unit_one)
        d_vec[6 * layer + 1] = column_sum(d_normed)
        d_stream = d_stream + norm_back(d_normed, unit_one, scale_one, gains[0])
    d_reward, d_state, d_move = (d_stream[k * slots : (k + 1) * slots] for k in range(3))
    d_times_ref[0:slots] = jnp.where(valid, d_reward + d_state + d_move, 0.0)
    d_reward = d_reward * (1.0 - reward * reward)
    d_vec[14] = column_sum(d_reward * amount)
    d_vec[15] = column_sum(d_reward)
    d_move = d_move * (1.0 - move * move)
    d_small_ref[24:48] = mm_tn(picks, d_move)[0:24]
    d_state = jnp.where(valid, d_state * (1.0 - state * state), 0.0)
    d_vec[16] = column_sum(d_state)
    d_small_ref[0:24] = jnp.concatenate(d_vec + [jnp.zeros((7, 128), F32)], axis=0)
    high, low = two_parts(d_state)
    twice = jnp.concatenate([high, high], axis=1)
    both = jnp.concatenate([high, low], axis=1)
    d_flat = dot_nt(twice, encoder[...]) + dot_nt(low, encoder[:, 0:128])
    d_block = dot_rows(flats[0, 0:slots], both) + dot_rows(flats[1, 0:slots], both)
    d_block = fold_pair(d_block)
    for k in range(28):
        z = jnp.where(valid, z_ref[k, 0:slots], 0.0)
        d_three_ref[k, 0:slots] = d_flat[:, k * 128 : (k + 1) * 128] * gelu_both(z)[1]
        y, v = divmod(k, 4)
        for o in range(2):
            if 2 * v + o < 7:
                d_encoder_ref[pl.ds(y * 7 + 2 * v + o, 64, stride=49), :] = d_block[
                    k * 128 + o * 64 : k * 128 + (o + 1) * 64
                ]


def former_kernel(
    packed,
    lengths_from,
    starts_from,
    index_from,
    returns_ref,
    actions_ref,
    z_from,
    flat_ref,
    *refs,
):
    if packed:
        split_ref, refs = refs[0], refs[1:]
    else:
        given, refs = refs[:5], refs[5:]
    (d_three_to, rows_ref), refs = refs[:2], refs[2:]
    if packed:
        parts, refs = refs[:8], refs[8:]
        (d_encoder_ref, d_small_ref, d_split), refs = refs[:3], refs[3:]
        weights, grads, refs = refs[:5], refs[5:10], refs[10:]
    else:
        (d_encoder_ref, d_small_ref), grads, refs = refs[:2], refs[2:7], refs[7:]
        weights = given
    (raw, near, small, rows_raw, times_all, encoder, chances, kept, sums, flats), refs = (
        refs[:10],
        refs[10:],
    )
    z_ref, d_three_ref, head_ref, lengths_ref, starts_ref, index_ref, sem = refs
    used = jnp.int32(0)
    wins = lengths_ref.shape[0]
    scalars = [
        pltpu.make_async_copy(source, target, sem.at[wins + 4 + number])
        for number, (source, target) in enumerate(
            ((lengths_from, lengths_ref), (starts_from, starts_ref), (index_from, index_ref))
        )
    ]
    for copy in scalars:
        copy.start()
    for copy in scalars:
        copy.wait()
    for w in range(wins):
        used = used + lengths_ref[w]

    def z_copy(slots):
        return pltpu.make_async_copy(
            z_from.at[:, pl.ds(0, slots)], z_ref.at[:, pl.ds(0, slots)], sem.at[wins + 3]
        )

    def z_back(slots):
        return pltpu.make_async_copy(
            d_three_ref.at[:, pl.ds(0, slots)], d_three_to.at[:, pl.ds(0, slots)], sem.at[wins + 3]
        )

    copies = [
        pltpu.make_async_copy(flat_ref.at[pl.ds(608, 3144)], raw, sem.at[0]),
        pltpu.make_async_copy(flat_ref.at[pl.ds(3744, 48)], rows_raw.at[wins], sem.at[1]),
        pltpu.make_async_copy(
            flat_ref.at[pl.ds(7872, 24)], rows_raw.at[wins + 1, pl.ds(0, 24)], sem.at[2]
        ),
    ]
    offsets = []
    for w in range(wins):
        row = TIME_ROW + starts_ref[w]
        low = pl.multiple_of(lax.div(row, 8) * 8, 8)
        offsets.append(row - low)
        copies.append(
            pltpu.make_async_copy(
                flat_ref.at[pl.ds(low, 40)], rows_raw.at[w, pl.ds(0, 40)], sem.at[3 + w]
            )
        )
    for copy in copies:
        copy.start()

    @pl.when(used <= HALF)
    def few_states():
        z_copy(HALF).start()

    @pl.when(used > HALF)
    def many_states():
        z_copy(ROOM).start()

    if packed:
        unpack_split(split_ref, *weights)
    for copy in copies:
        copy.wait()
    lane = lanes()

    def straight(first, second):
        return jnp.where(lane < 96, pltpu.roll(first, 96, 1), pltpu.roll(second, 96, 1))

    def turn(step, carry):
        spot = pl.multiple_of(step * 64, 64)
        near[pl.ds(spot, 64)] = straight(raw[pl.ds(spot + 1, 64)], raw[pl.ds(spot + 2, 64)])
        return carry

    lax.fori_loop(0, 49, turn, 0)
    for k in range(28):
        y, v = divmod(k, 4)
        halves = []
        for o in range(2):
            if 2 * v + o < 7:
                halves.append(near[pl.ds(y * 7 + 2 * v + o, 64, stride=49), :])
            else:
                halves.append(jnp.zeros((64, 128), F32))
        encoder[k * 128 : (k + 1) * 128] = pair(jnp.concatenate(halves, axis=0))
    small[...] = straight(rows_raw[wins, 1:41], rows_raw[wins, 2:42])
    head_ref[...] = square_head(
        straight(rows_raw[wins + 1, 4:22], rows_raw[wins + 1, 5:23])
    )
    times_all[...] = jnp.zeros(times_all.shape, F32)
    begin = 0
    row = lax.broadcasted_iota(jnp.int32, (32, 1), 0)
    for w in range(wins):
        rows = straight(
            rows_raw[w, pl.ds(offsets[w], 32)], rows_raw[w, pl.ds(offsets[w] + 1, 32)]
        )
        times_all[pl.ds(begin, 32)] = jnp.where(row < lengths_ref[w], rows, 0.0)
        begin = begin + lengths_ref[w]
    rows_ref[...] = jnp.zeros(rows_ref.shape, F32)
    note = jnp.zeros((1, 128), F32)
    for w in range(wins):
        note = jnp.where(lane == w, lengths_ref[w].astype(F32), note)
        note = jnp.where(lane == wins + w, starts_ref[w].astype(F32), note)
    rows_ref[ROOM : ROOM + 1] = note
    d_small_ref[...] = jnp.zeros(d_small_ref.shape, F32)

    def run(slots):
        z_copy(slots).wait()
        former_body(
            slots,
            used,
            lengths_ref,
            returns_ref,
            actions_ref,
            head_ref,
            z_ref,
            small,
            times_all,
            encoder,
            weights,
            d_three_ref,
            d_encoder_ref,
            d_small_ref,
            rows_ref,
            grads,
            chances,
            kept,
            sums,
            flats,
        )
        z_back(slots).start()

    @pl.when(used <= HALF)
    def few():
        run(HALF)

    @pl.when(used > HALF)
    def many():
        run(ROOM)

    if packed:
        count = d_small_ref.shape[0] // 4
        pack_split(d_split, *grads)
        for k in range(4):
            parts[k][...] = d_split[jnp.bitwise_xor(index_ref[0], k)]
            e = jnp.bitwise_xor(index_ref[1], k)
            held = d_encoder_ref[pl.ds(pl.multiple_of(e * 784, 8), 784)]
            parts[4 + k][0:784] = held
            held = d_small_ref[pl.ds(pl.multiple_of(e * count, 8), count)]
            parts[4 + k][784 : 784 + count] = held

    @pl.when(used <= HALF)
    def few_end():
        z_back(HALF).wait()

    @pl.when(used > HALF)
    def many_end():
        z_back(ROOM).wait()


def former(lengths, starts, index, returns, actions, z_three, flat, weights, small_rows, packed):
    vmem = pl.BlockSpec(memory_space=pltpu.VMEM)
    hbm = pl.BlockSpec(memory_space=pltpu.HBM)
    wins = lengths.shape[0]
    canonical = [
        (LAYERS, 3, 128, 128),
        (LAYERS, 128, 128),
        (LAYERS, 128, FF),
        (LAYERS, 1, FF),
        (LAYERS, FF, 128),
    ]
    outs, out_specs = [(28, ROOM, 128), (ROOM + 8, 128)], [hbm, vmem]
    if packed:
        outs += [(784, 128)] * 4 + [(784 + small_rows // 4, 128)] * 4
        out_specs += [vmem] * 8
        scratch = [
            pltpu.VMEM((3136, 128), F32),
            pltpu.VMEM((small_rows, 128), F32),
            pltpu.VMEM((4, 784, 128), F32),
        ]
        scratch += [pltpu.VMEM(shape, F32) for shape in canonical] * 2
    else:
        outs += [(3136, 128), (small_rows, 128)] + canonical
        out_specs += [vmem] * 7
        scratch = []
    rows = 3 * ROOM
    scratch += [
        pltpu.VMEM((3144, 128), F32),
        pltpu.VMEM((3136, 128), F32),
        pltpu.VMEM((40, 128), F32),
        pltpu.VMEM((wins + 2, 48, 128), F32),
        pltpu.VMEM((ROOM + 32, 128), F32),
        pltpu.VMEM((3584, 256), BF16),
        pltpu.VMEM((LAYERS, 2, 8 * rows, rows), BF16),
        pltpu.VMEM((LAYERS, 8, rows, 128), BF16),
        pltpu.VMEM((4, rows, 128), F32),
        pltpu.VMEM((2, ROOM, 3584), BF16),
        pltpu.VMEM((28, ROOM, 128), F32),
        pltpu.VMEM((28, ROOM, 128), F32),
        pltpu.VMEM((128, 128), F32),
        pltpu.SMEM((wins,), jnp.int32),
        pltpu.SMEM((wins,), jnp.int32),
        pltpu.SMEM((2,), jnp.int32),
        pltpu.SemaphoreType.DMA((wins + 7,)),
    ]
    return pl.pallas_call(
        partial(former_kernel, packed),
        in_specs=[hbm] * 3 + [vmem] * 2 + [hbm] * 2 + [vmem] * len(weights),
        out_specs=out_specs,
        out_shape=[jax.ShapeDtypeStruct(shape, F32) for shape in outs],
        scratch_shapes=scratch,
        compiler_params=pltpu.CompilerParams(vmem_limit_bytes=62 * 1024 * 1024),
        name="transformer_step",
    )(lengths, starts, index, returns, actions, z_three, flat, *weights)


SMALL = [("vectors", 24), ("action_table", 24), ("head", 24), ("loss", 8)]
FIELD_ROWS = 8200
EARLY_ROWS = CONV_ROWS + 3136
TABLE_AT = CONV_ROWS + 3136 + 17 + ACT


def round_up(number, grain):
    return -(-number // grain) * grain


def chunk_of(tiles):
    return max(size for size in range(1, 9) if tiles % size == 0)


def mesh_bits(dp_size, mp_size):
    dp_bits = [("dp", k) for k in range(dp_size.bit_length() - 1)]
    mp_bits = [("mp", k) for k in range(mp_size.bit_length() - 1)]
    middle = (len(dp_bits) - 1) // 2
    return mp_bits[:1], mp_bits[1:], dp_bits[:middle], dp_bits[middle:]


def reduce_kernel(plan, *refs):
    mp_size, quarter, share = plan["mp_size"], plan["quarter"], plan["share"]
    split_parts, own_parts, conv_ref = refs[:mp_size], refs[mp_size : 2 * mp_size], refs[2 * mp_size]
    refs = refs[2 * mp_size + 1 :]
    (early_out, small_out, split_out, square_out), refs = refs[:4], refs[4:]
    (split_stage, own_stage, work, landing, split_total, own_total, conv_total), refs = (
        refs[:7],
        refs[7:],
    )
    tiles, tile_in, load_sem, send_sem, recv_sem, store_sem = refs
    spots = {"dp": lax.axis_index("dp"), "mp": lax.axis_index("mp")}
    cores, ys, xs, zs = plan["bits"]
    slots = iter(range(plan["copies"]))

    def value(bit):
        return lax.rem(lax.div(spots[bit[0]], 1 << bit[1]), 2)

    def turned(stage, mask):
        index = 0
        for k, bit in enumerate(stage):
            own = value(bit)
            index = index + ((1 - own) if mask & (1 << k) else own) * (1 << k)
        return index

    def partner(stage, mask):
        place = dict(spots)
        for k, bit in enumerate(stage):
            if mask & (1 << k):
                place[bit[0]] = place[bit[0]] + (1 - 2 * value(bit)) * (1 << bit[1])
        return (place["dp"], place["mp"])

    def masks_of(stage):
        return range(1, 1 << len(stage))

    def send(source, target, stage, mask):
        slot = next(slots)
        copy = pltpu.make_async_remote_copy(
            src_ref=source,
            dst_ref=target,
            send_sem=send_sem.at[slot],
            recv_sem=recv_sem.at[slot],
            device_id=partner(stage, mask),
            device_id_type=pl.DeviceIdType.MESH,
        )
        copy.start()
        return copy

    loads = []
    for k in range(mp_size):
        for parts, stage in ((own_parts, own_stage), (split_parts, split_stage)):
            copy = pltpu.make_async_copy(parts[k], stage.at[k], load_sem.at[len(loads)])
            loads.append(copy)
    conv_tiles = CONV_ROWS // 8
    target = work.at[pl.ds(plan["conv"], conv_tiles)]
    loads.append(pltpu.make_async_copy(conv_ref, target, load_sem.at[len(loads)]))
    for load in loads:
        load.start()

    def wipe(target, start, count):
        if count > 0:
            target[start : start + count] = jnp.zeros((count, 8, 128), F32)

    wipe(work, plan["conv"] + conv_tiles, plan["conv_size"] - conv_tiles)
    wipe(work, plan["split"] + quarter, plan["split_size"] - quarter)
    wipe(work, plan["own"] + quarter + share, plan["own_size"] - quarter - share)
    barrier = pltpu.get_barrier_semaphore()
    greeted = [(stage, mask) for stage in (cores + ys, xs, zs) for mask in masks_of(stage)]
    for stage, mask in greeted:
        pl.semaphore_signal(
            barrier,
            inc=1,
            device_id=partner(stage, mask),
            device_id_type=pl.DeviceIdType.MESH,
        )
    pl.semaphore_wait(barrier, len(greeted))

    def sum_into(target, start, pieces, count):
        chunk = chunk_of(count)

        def body(turn, carry):
            held = pieces[0][0][pl.ds(pieces[0][1] + turn * chunk, chunk)]
            for source, at in pieces[1:]:
                held = held + source[pl.ds(at + turn * chunk, chunk)]
            target[pl.ds(start + turn * chunk, chunk)] = held
            return carry

        lax.fori_loop(0, count // chunk, body, 0)

    class Stream:
        def __init__(self, base, size, stages, total, total_at):
            self.base, self.size, self.stages = base, size, stages
            self.total, self.at = total, total_at
            self.land = base
            self.flight = None
            self.step = 0
            self.start = base

        def reduce(self):
            if self.flight is not None:
                copies, piece, lands, keep = self.flight
                for copy in copies:
                    copy.wait()
                pieces = [(work, keep)] + [(landing, land) for land in lands]
                sum_into(work, keep, pieces, piece)
                self.base, self.size, self.flight = keep, piece, None
            if self.step < len(self.stages):
                stage = self.stages[self.step]
                piece = self.size >> len(stage)
                keep = self.base + turned(stage, 0) * piece
                copies, lands = [], []
                for mask in masks_of(stage):
                    give = self.base + turned(stage, mask) * piece
                    target = landing.at[pl.ds(self.land, piece)]
                    copies.append(send(work.at[pl.ds(give, piece)], target, stage, mask))
                    lands.append(self.land)
                    self.land += piece
                self.flight = (copies, piece, lands, keep)
                self.step += 1

        def turn(self):
            self.at = self.at + (self.base - self.start)
            sum_into(self.total, self.at, [(work, self.base)], self.size)
            self.step = 0

        def double(self):
            if self.flight is not None:
                for copy in self.flight:
                    copy.wait()
                stage = self.stages[len(self.stages) - self.step]
                self.at = self.at - turned(stage, 0) * self.size
                self.size, self.flight = self.size << len(stage), None
            if self.step < len(self.stages):
                stage = self.stages[len(self.stages) - 1 - self.step]
                region = self.total.at[pl.ds(self.at, self.size)]
                self.flight = [send(region, region, stage, mask) for mask in masks_of(stage)]
                self.step += 1

        def squares(self, keep):
            held = work[pl.ds(self.base, self.size)]
            if keep is not None:
                tile = lax.broadcasted_iota(jnp.int32, (self.size, 8, 128), 0)
                held = jnp.where(keep(tile + self.base), held, 0.0)
            return jnp.sum(held * held, axis=0)

    sharing = cores + xs
    seat = sum(value(bit) * (1 << k) for k, bit in enumerate(sharing))

    def keep_own(tile):
        place = tile - plan["own"] - quarter
        return (place < 0) | (place + seat * share < 9)

    class Quarter:
        def __init__(self, stream, offset, stages):
            self.at = stream.base - stream.start + offset
            self.size, self.stages = stream.size, stages
            self.held, self.flights, self.step = [0], [], 0
            sum_into(own_total.at[seat], self.at, [(work, stream.base)], stream.size)

        def region(self, offset):
            return own_total.at[turned(sharing, offset), pl.ds(self.at, self.size)]

        def double(self):
            if self.flights:
                for copy in self.flights:
                    copy.wait()
                stage = self.stages[self.step - 1]
                if stage[0] in sharing:
                    changed = 1 << sharing.index(stage[0])
                    self.held = self.held + [offset | changed for offset in self.held]
                else:
                    self.at = self.at - turned(stage, 0) * self.size
                    self.size <<= len(stage)
                self.flights = []
            if self.step < len(self.stages):
                stage = self.stages[self.step]
                for offset in self.held:
                    region = self.region(offset)
                    self.flights += [send(region, region, stage, mask) for mask in masks_of(stage)]
                self.step += 1

    first, second = plan["cut"]
    own = [
        Stream(plan["own"], first, [ys, zs], None, 0),
        Stream(plan["own"] + first, plan["own_size"] - first, [zs, ys], None, 0),
    ]
    split = [
        Stream(plan["split"], second, [xs, zs], split_total, 0),
        Stream(
            plan["split"] + second,
            plan["split_size"] - second,
            [zs, xs],
            split_total,
            second,
        ),
    ]
    conv = Stream(plan["conv"], plan["conv_size"], [cores + ys, xs, zs], conv_total, 0)
    for load in loads:
        load.wait()
    sum_into(
        work,
        plan["own"],
        [(own_stage.at[k], 0) for k in range(mp_size)],
        quarter + share,
    )
    for stream in own + [conv]:
        stream.reduce()
    sum_into(work, plan["split"], [(split_stage.at[k], 0) for k in range(mp_size)], quarter)
    for stream in own + [conv]:
        stream.reduce()
    for stream in split:
        stream.reduce()
    for stream in own:
        stream.reduce()
    squares = jnp.zeros((8, 128), F32)
    singles = [[bit] for bit in xs]
    quarters = [
        Quarter(own[0], 0, [zs, ys] + singles + [cores]),
        Quarter(own[1], first, [ys] + singles + [zs, cores]),
    ]
    for piece in quarters:
        piece.double()
    conv.reduce()
    for stream in split:
        stream.reduce()
    for stream in own:
        squares = squares + stream.squares(keep_own)
    for piece in quarters:
        piece.double()
    conv.reduce()
    squares = squares + conv.squares(None)
    conv.turn()
    conv.double()
    for stream in split:
        stream.reduce()
        squares = squares + stream.squares(None)
    tiles[0] = squares
    tile_stages = [cores + ys, xs, zs]

    def send_tiles(number):
        stage = tile_stages[number]
        spot = number * 8 - 1
        return [
            send(tiles.at[number], tile_in.at[spot + mask], stage, mask)
            for mask in masks_of(stage)
        ]

    tile_flights = send_tiles(0)
    for stream in split:
        stream.turn()
        stream.double()
    rounds = 1
    while rounds <= len(tile_stages) or conv.flight is not None or quarters[0].flights:
        for stream in quarters + [conv]:
            stream.double()
        if rounds <= len(tile_stages):
            for copy in tile_flights:
                copy.wait()
            held = tiles[rounds - 1]
            for mask in masks_of(tile_stages[rounds - 1]):
                held = held + tile_in[(rounds - 1) * 8 - 1 + mask]
            tiles[rounds] = held
            if rounds < len(tile_stages):
                tile_flights = send_tiles(rounds)
        for stream in split:
            stream.double()
        rounds += 1
    square_out[...] = tiles[len(tile_stages)]
    stores = [
        (conv_total.at[pl.ds(0, conv_tiles)], early_out.at[pl.ds(0, conv_tiles)]),
        (split_total.at[pl.ds(0, quarter)], split_out),
    ]
    for m in range(mp_size):
        rows = pl.ds(conv_tiles + m * quarter, quarter)
        stores.append((own_total.at[m, pl.ds(0, quarter)], early_out.at[rows]))
        rows = pl.ds(m * share, share)
        stores.append((own_total.at[m, pl.ds(quarter, share)], small_out.at[rows]))
    stores = [
        pltpu.make_async_copy(source, target, store_sem.at[number])
        for number, (source, target) in enumerate(stores)
    ]
    for copy in stores:
        copy.start()
    for copy in stores:
        copy.wait()


def reduce_all(split_parts, own_parts, conv, dp_size, mp_size):
    bits = mesh_bits(dp_size, mp_size)
    quarter = split_parts[0].shape[0] // 8
    share = own_parts[0].shape[0] // 8 - quarter
    own_size = round_up(quarter + share, dp_size)
    split_size = round_up(quarter, dp_size)
    conv_size = round_up(CONV_ROWS // 8, dp_size * mp_size)
    places, at = {}, 0
    for name, size in [("split", split_size), ("own", own_size), ("conv", conv_size)]:
        places[name] = at
        at += size
    cut = (round_up(own_size // 2, dp_size), round_up(split_size // 2, dp_size))
    copies = 16 * (dp_size + mp_size) + 2 * mp_size * dp_size
    plan = dict(
        places,
        mp_size=mp_size,
        quarter=quarter,
        share=share,
        bits=bits,
        copies=copies,
        split_size=split_size,
        own_size=own_size,
        conv_size=conv_size,
        cut=cut,
    )
    vmem = pl.BlockSpec(memory_space=pltpu.VMEM)
    any_spec = pl.BlockSpec(memory_space=pl.ANY)
    arrays = [*split_parts, *own_parts, conv]
    loads = len(arrays)

    def tiled(size, *lead):
        return pltpu.VMEM((*lead, size, 8, 128), F32)

    outs = [(EARLY_ROWS // 8, 8, 128), (share * mp_size, 8, 128), (quarter, 8, 128), (8, 128)]
    results = pl.pallas_call(
        partial(reduce_kernel, plan),
        in_specs=[any_spec] * loads,
        out_specs=[any_spec, any_spec, any_spec, vmem],
        out_shape=[jax.ShapeDtypeStruct(shape, F32) for shape in outs],
        scratch_shapes=[
            tiled(quarter, mp_size),
            tiled(quarter + share, mp_size),
            tiled(at),
            tiled(at),
            tiled(split_size),
            tiled(own_size, mp_size),
            tiled(conv_size),
            pltpu.VMEM((4, 8, 128), F32),
            pltpu.VMEM((24, 8, 128), F32),
            pltpu.SemaphoreType.DMA((loads,)),
            pltpu.SemaphoreType.DMA((copies,)),
            pltpu.SemaphoreType.DMA((copies,)),
            pltpu.SemaphoreType.DMA((2 + 2 * mp_size,)),
        ],
        compiler_params=pltpu.CompilerParams(
            collective_id=1, has_side_effects=True, vmem_limit_bytes=62 * 1024 * 1024
        ),
        name="reduce_gradients",
    )(*[array.reshape(-1, 8, 128) for array in arrays])
    return [held.reshape(-1, 128) for held in results]


FLAT_ROWS = 7896
BLOCK_ROWS = 1024
LATE = 609
SPAN = 40


def adam_kernel(
    wins,
    early_ref,
    rows_ref,
    small_ref,
    split_ref,
    square_ref,
    weight_ref,
    first_ref,
    second_ref,
    split_weight_ref,
    split_first_ref,
    split_second_ref,
    new_ref,
    new_first_ref,
    new_second_ref,
    low_ref,
    split_new_ref,
    split_new_first_ref,
    split_new_second_ref,
    split_low_ref,
    scalar_ref,
    split_in,
    split_out,
    field,
    rows,
    notes,
    marks,
    pulled,
    factor_ref,
    pull_sem,
    load_sem,
    split_sem,
):
    step = pl.program_id(0)
    last = pl.num_programs(0) - 1
    lane = lax.broadcasted_iota(jnp.int32, (1, 128), 1)

    def pull(block, slot):
        start = pl.multiple_of(block * BLOCK_ROWS, BLOCK_ROWS)
        return pltpu.make_async_copy(
            field.at[pl.ds(start, BLOCK_ROWS + 8)], pulled.at[slot], pull_sem.at[slot]
        )

    def update(weights, first, second, grads):
        first = beta_first * first + (1 - beta_first) * grads
        second = beta_second * second + (1 - beta_second) * grads * grads
        fix_one = 1.0 / (1 - beta_first**STEP)
        fix_two = 1.0 / (1 - beta_second**STEP)
        weights = weights - learn_rate * (
            first * fix_one / (jnp.sqrt(second * fix_two) + adam_epsilon) + weight_decay * weights
        )
        return weights, first, second

    def sum_of(tile):
        held = jnp.sum(jnp.sum(tile, axis=0, keepdims=True), axis=1, keepdims=True)
        return jnp.broadcast_to(held, (1, 128))

    slot = lax.rem(step, 2)
    split_loads = [
        pltpu.make_async_copy(ref, split_in.at[k], split_sem.at[k])
        for k, ref in enumerate((split_weight_ref, split_first_ref, split_second_ref))
    ]
    split_stores = [
        pltpu.make_async_copy(split_out.at[k], ref, split_sem.at[3 + k])
        for k, ref in enumerate((split_new_ref, split_new_first_ref, split_new_second_ref))
    ]

    @pl.when(step == 0)
    def prepare():
        for load in split_loads:
            load.start()
        load_rows = pltpu.make_async_copy(rows_ref, rows, load_sem.at[0])
        load_early = pltpu.make_async_copy(
            early_ref, field.at[pl.ds(0, EARLY_ROWS)], load_sem.at[1]
        )
        load_rows.start()
        load_early.start()
        late = FIELD_ROWS - EARLY_ROWS
        field[EARLY_ROWS:FIELD_ROWS] = jnp.zeros((late, 128), F32)
        load_rows.wait()
        stride = ROOM + 8
        devices = rows.shape[0] // stride
        notes[...] = rows[pl.ds(ROOM, devices, stride=stride), :]
        mark = pltpu.make_async_copy(notes, marks, load_sem.at[2])
        mark.start()
        mark.wait()
        place = lax.broadcasted_iota(jnp.int32, (SPAN, ROOM), 0)
        slot_of = lax.broadcasted_iota(jnp.int32, (SPAN, ROOM), 1)

        def scatter(turn, carry):
            spots, found = [], []
            for k in range(4):
                device = turn * 4 + k
                begin = jnp.int32(0)
                picks = []
                for w in range(wins):
                    length = marks[device, w].astype(jnp.int32)
                    row = marks[device, wins + w].astype(jnp.int32) + TABLE_AT
                    low = lax.div(row, 8) * 8
                    inside = (slot_of >= begin) & (slot_of < begin + length)
                    inside = inside & (place - slot_of == row - low - begin)
                    picks.append(jnp.where(inside, 1.0, 0.0).astype(BF16))
                    spots.append(low)
                    begin = begin + length
                held = pair(rows[pl.ds(pl.multiple_of(device * stride, 8), ROOM)])
                found.append(fold_pair(dot(jnp.concatenate(picks, axis=0), held)))
            for k in range(4):
                for w in range(wins):
                    spot = pl.ds(pl.multiple_of(spots[k * wins + w], 8), SPAN)
                    field[spot] = field[spot] + found[k][w * SPAN : (w + 1) * SPAN]
            return carry

        lax.fori_loop(0, devices // 4, scatter, 0)

        def fold(turn, carry):
            spot = pl.multiple_of(EARLY_ROWS + turn * 64, 8)
            held = field[pl.ds(spot, 64)]
            return carry + jnp.sum((held * held).reshape(8, 8, 128), axis=0)

        squares = lax.fori_loop(0, late // 64, fold, square_ref[...])
        at = EARLY_ROWS
        for name_at, count in [(0, 17), (24, ACT)]:
            field[at : at + count] = small_ref[name_at : name_at + count]
            at += count
        at = TABLE_AT + TSTEPS
        field[at : at + ACT] = small_ref[48 : 48 + ACT]
        lane_all = lax.broadcasted_iota(jnp.int32, notes.shape, 1)
        count = sum_of(jnp.where(lane_all < wins, notes[...], 0.0))
        seed = 1.0 / count
        norm = jnp.sqrt(sum_of(squares)) * seed
        factor = jnp.minimum(1.0, clip_limit / (norm + 1e-06)) * seed
        factor_ref[...] = jnp.broadcast_to(factor, (8, 128))
        loss = small_ref[72:73]
        row = lax.broadcasted_iota(jnp.int32, (8, 128), 0)
        scalar_ref[...] = jnp.where(row == 0, norm, jnp.where(row == 1, loss, count))
        load_early.wait()
        pull(0, 0).start()

    @pl.when(step < last)
    def ahead():
        pull(step + 1, 1 - slot).start()

    @pl.when(step == 1)
    def split():
        for load in split_loads:
            load.wait()
        count = split_in.shape[1]
        outs = update(*[split_in[k] for k in range(3)], split_ref[0:count] * factor_ref[0:1])
        for k in range(3):
            split_out[k] = outs[k]
        split_low_ref[...] = outs[0].astype(BF16)
        for store in split_stores:
            store.start()

    @pl.when(step == last)
    def split_end():
        for store in split_stores:
            store.wait()

    pull(step, slot).wait()
    early = pulled[slot, 0:BLOCK_ROWS]
    own = pltpu.roll(pulled[slot, 7 : BLOCK_ROWS + 7], 32, 1)
    before = pltpu.roll(pulled[slot, 6 : BLOCK_ROWS + 6], 32, 1)
    row = lax.broadcasted_iota(jnp.int32, (BLOCK_ROWS, 1), 0) + step * BLOCK_ROWS
    grads = jnp.where(lane < 32, jnp.where(row == LATE, early, before), own)
    grads = jnp.where(row < LATE, early, grads)
    outs = update(weight_ref[...], first_ref[...], second_ref[...], grads * factor_ref[0:1])
    new_ref[...], new_first_ref[...], new_second_ref[...] = outs
    low_ref[...] = outs[0].astype(BF16)


def adam_all(early, rows, small, split_grad, square, shared, split, wins):
    grid = -(-FLAT_ROWS // BLOCK_ROWS)
    flat_spec = pl.BlockSpec((BLOCK_ROWS, 128), lambda i: (i, 0))
    split_rows = split[0].shape[0]
    devices = rows.shape[0]

    def whole(shape):
        return pl.BlockSpec(shape, lambda i: (0,) * len(shape))

    shared_out = jax.ShapeDtypeStruct((FLAT_ROWS, 128), F32)
    split_out = jax.ShapeDtypeStruct((split_rows, 128), F32)
    any_spec = pl.BlockSpec(memory_space=pl.ANY)
    return pl.pallas_call(
        partial(adam_kernel, wins),
        grid=(grid,),
        in_specs=[
            any_spec,
            any_spec,
            whole(small.shape),
            whole(split_grad.shape),
            whole((8, 128)),
            flat_spec,
            flat_spec,
            flat_spec,
            any_spec,
            any_spec,
            any_spec,
        ],
        out_specs=[flat_spec] * 4
        + [any_spec] * 3
        + [whole((split_rows, 128)), whole((8, 128))],
        out_shape=[shared_out] * 3
        + [jax.ShapeDtypeStruct((FLAT_ROWS, 128), BF16)]
        + [split_out] * 3
        + [jax.ShapeDtypeStruct((split_rows, 128), BF16)]
        + [jax.ShapeDtypeStruct((8, 128), F32)],
        scratch_shapes=[
            pltpu.VMEM((3, split_rows, 128), F32),
            pltpu.VMEM((3, split_rows, 128), F32),
            pltpu.VMEM((FIELD_ROWS, 128), F32),
            pltpu.VMEM((devices * (ROOM + 8), 128), F32),
            pltpu.VMEM((devices, 128), F32),
            pltpu.SMEM((devices, 128), F32),
            pltpu.VMEM((2, BLOCK_ROWS + 8, 128), F32),
            pltpu.VMEM((8, 128), F32),
            pltpu.SemaphoreType.DMA((2,)),
            pltpu.SemaphoreType.DMA((3,)),
            pltpu.SemaphoreType.DMA((6,)),
        ],
        compiler_params=pltpu.CompilerParams(vmem_limit_bytes=62 * 1024 * 1024),
        name="adam_update",
    )(
        early,
        rows.reshape(devices * (ROOM + 8), 128),
        small,
        split_grad,
        square,
        *shared,
        *split,
    )


def per_device(
    frames,
    returns,
    actions,
    starts,
    lengths,
    shared_weights,
    shared_first,
    shared_second,
    split_weights,
    split_first,
    split_second,
):
    dp_size, mp_size = lax.axis_size("dp"), lax.axis_size("mp")
    narrow = D // mp_size
    hidden_width = FF // mp_size
    wins, steps = returns.shape
    width = split_weights.shape[0]
    split_rows = width // 128
    packed = narrow == 32
    own_rows = split_weights.reshape(split_rows, 128)
    split_all = lax.all_gather(own_rows, "mp", axis=0)
    flat = shared_weights.reshape(FLAT_ROWS, 128)
    picked, z_one, z_two, z_three = conv_forward(lengths, frames, flat)
    if packed:
        weights = [split_all]
    else:
        layers, layers_back = jax.vjp(
            lambda held: assemble(held, mp_size, narrow, hidden_width), split_all.reshape(-1)
        )
        weights = [
            jnp.stack([layer["qkv"].transpose(1, 0, 2) for layer in layers]),
            jnp.stack([layer["output"] for layer in layers]),
            jnp.stack([layer["up"] for layer in layers]),
            jnp.stack([layer["up_bias"][None] for layer in layers]),
            jnp.stack([layer["down"] for layer in layers]),
        ]
    small_rows = round_up(sum(rows for name, rows in SMALL), 8 * mp_size)
    cores, ys, xs, zs = mesh_bits(dp_size, mp_size)
    seat = jnp.bitwise_and(lax.axis_index("mp"), 1)
    seat = seat + 2 * jnp.bitwise_and(lax.axis_index("dp"), (1 << len(xs)) - 1)
    index = jnp.stack([lax.axis_index("mp"), seat])
    results = former(
        lengths, starts, index, returns, actions, z_three, flat, weights, small_rows, packed
    )
    d_three, rows = results[:2]
    rows_all = lax.all_gather(rows, ("dp", "mp"), axis=0)
    quarter = 3136 // mp_size
    if packed:
        split_parts, own_parts = results[2:6], results[6:]
    else:
        d_encoder, d_small, d_qkv, d_output, d_up, d_up_bias, d_down = results[2:]
        grad_layers = [
            dict(
                qkv=d_qkv[layer].transpose(1, 0, 2),
                output=d_output[layer],
                up=d_up[layer],
                up_bias=d_up_bias[layer, 0],
                down=d_down[layer],
            )
            for layer in range(LAYERS)
        ]
        gathered = layers_back(grad_layers)[0].reshape(mp_size, split_rows, 128)
        gathered = jnp.pad(gathered, ((0, 0), (0, quarter - split_rows), (0, 0)))
        encoder = d_encoder.reshape(mp_size, quarter, 128)
        small = d_small.reshape(mp_size, -1, 128)
        every = jnp.concatenate([encoder, small], axis=1)

        def turned(held, own):
            return [
                lax.dynamic_index_in_dim(held, jnp.bitwise_xor(own, k), 0, keepdims=False)
                for k in range(mp_size)
            ]

        split_parts, own_parts = turned(gathered, index[0]), turned(every, index[1])
    split_parts, own_parts = list(split_parts), list(own_parts)
    for k in range(1, mp_size):
        turn = [(place, place ^ k) for place in range(mp_size)]
        split_parts[k] = lax.ppermute(split_parts[k], "mp", turn)
        turn = [
            (dp * mp_size + mp, (dp ^ (k >> 1)) * mp_size + (mp ^ (k & 1)))
            for dp in range(dp_size)
            for mp in range(mp_size)
        ]
        own_parts[k] = lax.ppermute(own_parts[k], ("dp", "mp"), turn)
    d_conv = conv_backward(lengths, picked, z_one, z_two, d_three, flat)
    early, small, split_sum, square = reduce_all(
        split_parts, own_parts, d_conv, dp_size, mp_size
    )
    shared_view = [a.reshape(FLAT_ROWS, 128) for a in (shared_weights, shared_first, shared_second)]
    split_view = [a.reshape(split_rows, 128) for a in (split_weights, split_first, split_second)]
    updated = adam_all(
        early, rows_all, small, split_sum, square, shared_view, split_view, wins
    )
    shared_out = [a.reshape(-1) for a in updated[:4]]
    split_out = [a.reshape(-1) for a in updated[4:8]]
    scalars = updated[8]
    return (*shared_out, *split_out, scalars[0, 0], scalars[1, 0], scalars[2, 0])


def solution(mesh):
    return jax.shard_map(
        per_device,
        mesh=mesh,
        in_specs=(
            P(("dp", "mp"), None, None, None, None),
            P(("dp", "mp"), None),
            P(("dp", "mp"), None),
            P(("dp", "mp")),
            P(("dp", "mp")),
            P(),
            P(),
            P(),
            P("mp"),
            P("mp"),
            P("mp"),
        ),
        out_specs=(P(), P(), P(), P(), P("mp"), P("mp"), P("mp"), P("mp"), P(), P(), P()),
        check_vma=False,
    )
```

profile of v0, /device:TPU:0, one launch (start us, length us, event | category | flops | bytes accessed | tf_op | source)
XLA Modules:
  0.0 182.6 jit_solution(8771230429740062744)
XLA Ops:
  7.2 0.0 all-gather.4.cloned.1.call-start
  7.2 0.7 all-gather.4.cloned.1.call-update
  7.9 0.0 all-gather.6.cloned.1.call-start
  8.0 8.9 %conv_forward.1 = (bf16[8,21,4,16,640]{4,3,2,1,0:T(8,128)(2,1)}, f32[8,10,2,5,16,128]{5,4,3,2,1,0:T(8,128)}, f32[8,9,5,16,128]{4,3,2,1,0:T(8,128)}, f32[28,128,128]{2,1,0:T(8,128)}) custom-call(s32[4]{0:T(128)} %lengths_from.5, bf16[4,30,84,4,84]{4,3,2,1,0:T(4,128)(2,1)} %bitcast.37, f32[7896,128]{1,0:T(8,128)} %bitcast.33), custom_call_target="tpu_custom_call" | custom-call | tf_op jit(solution)/shard_map/conv_forward/pallas_call | solution.py:366
  16.8 0.6 pad_add_fusion.index_from
  17.4 14.6 %all-gather.4.cloned.1.call-done.refs_0_ = f32[4,770,128]{2,1,0:T(8,128)} async-done(((f32[1,770,128]{2,1,0:T(8,128)}), f32[4,770,128]{2,1,0:T(8,128)}) %all-gather.4.cloned.1.call-update) | async-done | bytes 1576976 | tf_op jit(solution)/shard_map/all_gather | solution.py:1952
  32.1 31.8 %transformer_step.1 = (f32[28,128,128]{2,1,0:T(8,128)}, f32[136,128]{1,0:T(8,128)}, f32[784,128]{1,0:T(8,128)}, f32[784,128]{1,0:T(8,128)}, f32[784,128]{1,0:T(8...) custom-call(s32[4]{0:T(128)} %lengths_from.5, ...), custom_call_target="tpu_custom_call" | custom-call | tf_op jit(solution)/shard_map/transformer_step/pallas_call | solution.py:1311
  63.9 0.0 all-gather.6.cloned.1.call-update
  63.9 0.3 collective-permute-start
  64.2 0.3 collective-permute-start.3
  64.5 1.5 collective-permute-start.4
  65.9 0.1 collective-permute-start.5
  66.1 0.4 collective-permute-start.1
  66.5 0.0 collective-permute-done
  66.5 0.0 copy-start.3
  66.5 1.5 collective-permute-start.2
  68.0 12.6 %conv_backward.1 = f32[616,128]{1,0:T(8,128)} custom-call(s32[4]{0:T(128)} %lengths_from.5, bf16[8,21,4,16,640]{4,3,2,1,0:T(8,128)(2,1)} %get-tuple-element.47.picked_ref, f32[8,10,2,5,16,128]{5,4,3,2,1,0:T(8,128)} %get-tuple-element.48.z_one_ref, f32[8,9,5,16,128]{4,3,2,1,0:T(8,128)} %get-tuple-element.49.z_two_ref, ...), custom_call_target="tpu_custom_call" | custom-call | tf_op jit(solution)/shard_map/conv_backward/pallas_call | solution.py:675
  80.6 0.0 copy-done.3
  80.6 0.0 collective-permute-done.1
  80.6 6.3 %collective-permute-done.2 = f32[784,128]{1,0:T(8,128)} collective-permute-done((f32[784,128]{1,0:T(8,128)}, f32[784,128]{1,0:T(8,128)}, u32[]{:S(2)}, u32[]{:S(2)}) %collective-permute-start.2) | collective-permute-done | bytes 401440 | tf_op jit(solution)/shard_map/ppermute | solution.py:2009
  86.9 0.0 collective-permute-done.3
  86.9 0.0 copy-start
  86.9 0.0 collective-permute-done.4
  86.9 0.0 copy-start.1
  86.9 0.0 collective-permute-done.5
  86.9 0.0 copy-start.2
  87.0 0.7 copy-done
  87.7 0.1 copy-done.1
  87.8 0.1 copy-done.2
  87.9 66.3 %reduce_gradients.1 = (f32[469,8,128]{2,1,0:T(8,128)}, f32[12,8,128]{2,1,0:T(8,128)}, f32[98,8,128]{2,1,0:T(8,128)}, f32[8,128]{1,0:T(8,128)}) custom-call(f32[98,8,128]{2,1,0:T(8,128)} %bitcast.48, f32[98,8,128]{2,1,0:T(8,128)} %bitcast.49, f32[98,8,128]{2,1,0:T(8,128)} %bitcast.7.refs_2_, f32[98,8,128]{2,1,0:T(8,128)} %bitcast.8.refs_3_, ...), custom_call_target="tpu_custom_call" | custom-call | tf_op jit(solution)/shard_map/reduce_gradients/pallas_call | solution.py:1663
  154.3 0.0 all-gather.6.cloned.1.call-done.rows_ref
  154.3 20.2 %adam_update.1 = (f32[7896,128]{1,0:T(8,128)}, f32[7896,128]{1,0:T(8,128)}, f32[7896,128]{1,0:T(8,128)}, bf16[7896,128]{1,0:T(8,128)(2,1)}, f32[770,128]{1,0:T(8...) custom-call(f32[3752,128]{1,0:T(8,128)} %bitcast.40, ...), custom_call_target="tpu_custom_call" | custom-call | tf_op jit(solution)/shard_map/adam_update/pallas_call | solution.py:1881
  174.5 1.3 fusion
Async XLA Ops:
  7.2 24.9 %all-gather.4.cloned.1.call-start = ((), (), s32[]{:S(2)}) async-start(), calls=%async_computation | async-start | bytes 1986560 | tf_op jit(solution)/shard_map/all_gather | solution.py:1952
  7.9 146.4 %all-gather.6.cloned.1.call-start = ((), (), s32[]{:S(2)}) async-start(), calls=%async_computation.1 | async-start | bytes 2297856 | tf_op jit(solution)/shard_map/all_gather | solution.py:1977
  63.9 2.6 %collective-permute-start = (f32[784,128]{1,0:T(8,128)}, f32[784,128]{1,0:T(8,128)S(1)}, u32[]{:S(2)}, u32[]{:S(2)}) collective-permute-start(f32[784,128]{1,0:T(8,128)} %get-tuple-element.40), channel_id=1, source_target_pairs={{0,1},{1,0},{2,3},{3,2},{4,5},{5,4},{6,7},{7,6},{8,9},{9,8},{10,11... | collective-permute-start | bytes 1204232 | tf_op jit(solution)/shard_map/ppermute | solution.py:2009
  64.2 22.7 %collective-permute-start.3 = (f32[808,128]{1,0:T(8,128)}, f32[808,128]{1,0:T(8,128)S(1)}, u32[]{:S(2)}, u32[]{:S(2)}) collective-permute-start(f32[808,128]{1,0:T(8,128)} %get-tuple-element.44), channel_id=1, source_target_pairs={{0,1},{1,0},{2,3},{3,2},{4,5},{5,4},{6,7},{7,6},{8,9},{9,8},{10,11... | collective-permute-start | bytes 1241096 | tf_op jit(solution)/shard_map/ppermute | solution.py:2015
  64.5 22.4 %collective-permute-start.4 = (f32[808,128]{1,0:T(8,128)}, f32[808,128]{1,0:T(8,128)S(1)}, u32[]{:S(2)}, u32[]{:S(2)}) collective-permute-start(f32[808,128]{1,0:T(8,128)} %get-tuple-element.45), channel_id=1, source_target_pairs={{0,4},{1,5},{2,6},{3,7},{4,0},{5,1},{6,2},{7,3},{8,12},{9,13},{10,... | collective-permute-start | bytes 1241096 | tf_op jit(solution)/shard_map/ppermute | solution.py:2015
  65.9 21.0 %collective-permute-start.5 = (f32[808,128]{1,0:T(8,128)}, f32[808,128]{1,0:T(8,128)S(1)}, u32[]{:S(2)}, u32[]{:S(2)}) collective-permute-start(f32[808,128]{1,0:T(8,128)} %get-tuple-element.46), channel_id=1, source_target_pairs={{0,5},{1,4},{2,7},{3,6},{4,1},{5,0},{6,3},{7,2},{8,13},{9,12},{10,... | collective-permute-start | bytes 1241096 | tf_op jit(solution)/shard_map/ppermute | solution.py:2015
  66.1 14.5 %collective-permute-start.1 = (f32[784,128]{1,0:T(8,128)}, f32[784,128]{1,0:T(8,128)}, u32[]{:S(2)}, u32[]{:S(2)}) collective-permute-start(f32[784,128]{1,0:T(8,128)} %get-tuple-element.41), channel_id=1, source_target_pairs={{0,2},{1,3},{2,0},{3,1},{4,6},{5,7},{6,4},{7,5},{8,10},{9,11},{10,... | collective-permute-start | bytes 1204232 | tf_op jit(solution)/shard_map/ppermute | solution.py:2009
  66.5 14.1 %copy-start.3 = (f32[784,128]{1,0:T(8,128)}, f32[784,128]{1,0:T(8,128)S(1)}, u32[]{:S(2)}) copy-start(f32[784,128]{1,0:T(8,128)S(1)} %collective-permute-done) | copy-start | bytes 1204228
  66.5 20.4 %collective-permute-start.2 = (f32[784,128]{1,0:T(8,128)}, f32[784,128]{1,0:T(8,128)}, u32[]{:S(2)}, u32[]{:S(2)}) collective-permute-start(f32[784,128]{1,0:T(8,128)} %get-tuple-element.42), channel_id=1, source_target_pairs={{0,3},{1,2},{2,1},{3,0},{4,7},{5,6},{6,5},{7,4},{8,11},{9,10},{10,... | collective-permute-start | bytes 1204232 | tf_op jit(solution)/shard_map/ppermute | solution.py:2009
  86.9 0.8 copy-start
  86.9 0.9 copy-start.1
  86.9 1.0 copy-start.2
Sparse Core Ops, SparseCore 0:
  9.6 22.4 all-gather.3
  64.0 66.1 all-gather.5
where the time goes:
time: 185 us; the launch traced here: 183 us
  Pallas kernels  140 us (76%)
  waiting for transfers between devices  21.7 us (12%)
  between operations  14.2 us (8%)
  starting transfers between devices  4.14 us (2%)
  local copies, waits for them, and re-layouts  2.3 us (1%)
    pallas_call x1, Pallas kernels, reduce_all(): pl.pallas_call(partial(reduce_kernel, plan), in_specs=[any_spec] * loads,...  66.3 us
    pallas_call x1, Pallas kernels, former(): pl.pallas_call(partial(former_kernel, packed), in_specs=[hbm] * 3 + [vmem...  31.8 us
    pallas_call x1, Pallas kernels, adam_all(): pl.pallas_call(partial(adam_kernel, wins), grid=(grid,), in_specs=[any_sp...  20.2 us
    all_gather x1, waiting for transfers between devices, per_device(): split_all = lax.all_gather(own_rows, 'mp', axis=0)  14.6 us
    pallas_call x1, Pallas kernels, conv_backward(): pl.pallas_call(conv_backward_kernel, in_specs=[hbm] * 6, out_specs=vmem,...  12.6 us
    pallas_call x1, Pallas kernels, conv_forward(): pl.pallas_call(conv_forward_kernel, in_specs=[any_spec, any_spec, any_spe...  8.85 us
    ppermute x3, waiting for transfers between devices, per_device(): split_parts[k] = lax.ppermute(split_parts[k], 'mp', turn)  6.33 us
  transfers between devices with their start and end apart: 8, of which 2 were waited for; matrix products, arithmetic and copies ran while one was open for 0% of the time, Pallas kernels for 48%

commit v1 on v0

--- a/solution.py
+++ b/solution.py
@@ -63,6 +63,7 @@
 
 GROUP = 16
 CONV_ROWS = 616
+FAST_ROWS = 768
 ROOM = 128
 HALF = 64
 BF16 = jnp.bfloat16
@@ -488,12 +489,16 @@
 
 def conv_backward_kernel(
     lengths_from,
+    index_from,
+    table_ref,
+    times_ref,
     picked_ref,
     z_one_ref,
     z_two_ref,
     d_three_ref,
     shared_ref,
     flat_out,
+    flag_out,
     flat_ref,
     picked,
     z_one,
@@ -514,13 +519,16 @@
     total_one,
     total_two,
     total_three,
+    field,
     lengths_ref,
+    index_ref,
     load_sem,
     weight_sem,
 ):
-    scalars = pltpu.make_async_copy(lengths_from, lengths_ref, weight_sem)
-    scalars.start()
-    scalars.wait()
+    for source, target in ((lengths_from, lengths_ref), (index_from, index_ref)):
+        scalars = pltpu.make_async_copy(source, target, weight_sem)
+        scalars.start()
+        scalars.wait()
     used = jnp.int32(0)
     for w in range(lengths_ref.shape[0]):
         used = used + lengths_ref[w]
@@ -667,16 +675,30 @@
     flat_out[608:609] = flat_out[608:609] + jnp.where(lane >= 96, late, 0.0)
     row = lax.broadcasted_iota(jnp.int32, (7, 128), 0)
     flat_out[609:616] = jnp.where((row == 0) & (lane < 32), late, 0.0)
-
-
-def conv_backward(lengths, picked, z_one, z_two, d_three, flat):
+    wins = lengths_ref.shape[0]
+    shape = table_ref.shape
+    row = lax.broadcasted_iota(jnp.int32, shape, 0)
+    lane = lax.broadcasted_iota(jnp.int32, shape, 1)
+    counts = jnp.where(jnp.bitwise_and(lane, 2 * wins - 1) < wins, table_ref[...], 0.0)
+    ahead = (row < index_ref[2]) | ((row == index_ref[2]) & (lane < index_ref[0] * (2 * wins)))
+    before = jnp.sum(jnp.where(ahead, counts, 0.0)).astype(jnp.int32)
+    flag_out[0] = jnp.sum(counts).astype(jnp.int32)
+    field[...] = jnp.zeros(field.shape, F32)
+    field[pl.ds(jnp.minimum(before, FAST_ROWS), ROOM)] = times_ref[...]
+    flat_out[CONV_ROWS : CONV_ROWS + FAST_ROWS] = field[0:FAST_ROWS]
+
+
+def conv_backward(lengths, index, table, times, picked, z_one, z_two, d_three, flat):
     hbm = pl.BlockSpec(memory_space=pltpu.HBM)
     vmem = pl.BlockSpec(memory_space=pltpu.VMEM)
     return pl.pallas_call(
         conv_backward_kernel,
-        in_specs=[hbm] * 6,
-        out_specs=vmem,
-        out_shape=jax.ShapeDtypeStruct((CONV_ROWS, 128), F32),
+        in_specs=[hbm] * 2 + [vmem] * 2 + [hbm] * 5,
+        out_specs=[vmem, pl.BlockSpec(memory_space=pltpu.SMEM)],
+        out_shape=[
+            jax.ShapeDtypeStruct((CONV_ROWS + FAST_ROWS, 128), F32),
+            jax.ShapeDtypeStruct((1,), jnp.int32),
+        ],
         scratch_shapes=[
             pltpu.VMEM((CONV_ROWS, 128), F32),
             pltpu.VMEM((2, 21, 4, GROUP, 640), BF16),
@@ -698,13 +720,15 @@
             pltpu.VMEM((256, 1024), F32),
             pltpu.VMEM((256, 1024), F32),
             pltpu.VMEM((256, 768), F32),
+            pltpu.VMEM((FAST_ROWS + ROOM, 128), F32),
             pltpu.SMEM(lengths.shape, jnp.int32),
+            pltpu.SMEM((3,), jnp.int32),
             pltpu.SemaphoreType.DMA((2, 4)),
             pltpu.SemaphoreType.DMA,
         ],
         compiler_params=pltpu.CompilerParams(vmem_limit_bytes=62 * 1024 * 1024),
         name="conv_backward",
-    )(lengths, picked, z_one, z_two, d_three, flat)
+    )(lengths, index, table, times, picked, z_one, z_two, d_three, flat)
 
 
 HIGH = lax.Precision.HIGH
@@ -1202,11 +1226,6 @@
         times_all[pl.ds(begin, 32)] = jnp.where(row < lengths_ref[w], rows, 0.0)
         begin = begin + lengths_ref[w]
     rows_ref[...] = jnp.zeros(rows_ref.shape, F32)
-    note = jnp.zeros((1, 128), F32)
-    for w in range(wins):
-        note = jnp.where(lane == w, lengths_ref[w].astype(F32), note)
-        note = jnp.where(lane == wins + w, starts_ref[w].astype(F32), note)
-    rows_ref[ROOM : ROOM + 1] = note
     d_small_ref[...] = jnp.zeros(d_small_ref.shape, F32)
 
     def run(slots):
@@ -1274,7 +1293,7 @@
         (LAYERS, 1, FF),
         (LAYERS, FF, 128),
     ]
-    outs, out_specs = [(28, ROOM, 128), (ROOM + 8, 128)], [hbm, vmem]
+    outs, out_specs = [(28, ROOM, 128), (ROOM, 128)], [hbm, vmem]
     if packed:
         outs += [(784, 128)] * 4 + [(784 + small_rows // 4, 128)] * 4
         out_specs += [vmem] * 8
@@ -1305,7 +1324,7 @@
         pltpu.VMEM((128, 128), F32),
         pltpu.SMEM((wins,), jnp.int32),
         pltpu.SMEM((wins,), jnp.int32),
-        pltpu.SMEM((2,), jnp.int32),
+        pltpu.SMEM((3,), jnp.int32),
         pltpu.SemaphoreType.DMA((wins + 7,)),
     ]
     return pl.pallas_call(
@@ -1344,7 +1363,7 @@
     mp_size, quarter, share = plan["mp_size"], plan["quarter"], plan["share"]
     split_parts, own_parts, conv_ref = refs[:mp_size], refs[mp_size : 2 * mp_size], refs[2 * mp_size]
     refs = refs[2 * mp_size + 1 :]
-    (early_out, small_out, split_out, square_out), refs = refs[:4], refs[4:]
+    (early_out, times_out, small_out, split_out, square_out), refs = refs[:5], refs[5:]
     (split_stage, own_stage, work, landing, split_total, own_total, conv_total), refs = (
         refs[:7],
         refs[7:],
@@ -1392,8 +1411,8 @@
         for parts, stage in ((own_parts, own_stage), (split_parts, split_stage)):
             copy = pltpu.make_async_copy(parts[k], stage.at[k], load_sem.at[len(loads)])
             loads.append(copy)
-    conv_tiles = CONV_ROWS // 8
-    target = work.at[pl.ds(plan["conv"], conv_tiles)]
+    conv_tiles, time_tiles = CONV_ROWS // 8, FAST_ROWS // 8
+    target = work.at[pl.ds(plan["conv"], conv_tiles + time_tiles)]
     loads.append(pltpu.make_async_copy(conv_ref, target, load_sem.at[len(loads)]))
     for load in loads:
         load.start()
@@ -1402,7 +1421,8 @@
         if count > 0:
             target[start : start + count] = jnp.zeros((count, 8, 128), F32)
 
-    wipe(work, plan["conv"] + conv_tiles, plan["conv_size"] - conv_tiles)
+    filled = conv_tiles + time_tiles
+    wipe(work, plan["conv"] + filled, plan["conv_size"] - filled)
     wipe(work, plan["split"] + quarter, plan["split_size"] - quarter)
     wipe(work, plan["own"] + quarter + share, plan["own_size"] - quarter - share)
     barrier = pltpu.get_barrier_semaphore()
@@ -1569,7 +1589,7 @@
     for piece in quarters:
         piece.double()
     conv.reduce()
-    squares = squares + conv.squares(None)
+    squares = squares + conv.squares(lambda tile: tile - plan["conv"] < conv_tiles)
     conv.turn()
     conv.double()
     for stream in split:
@@ -1609,6 +1629,7 @@
     square_out[...] = tiles[len(tile_stages)]
     stores = [
         (conv_total.at[pl.ds(0, conv_tiles)], early_out.at[pl.ds(0, conv_tiles)]),
+        (conv_total.at[pl.ds(conv_tiles, time_tiles)], times_out),
         (split_total.at[pl.ds(0, quarter)], split_out),
     ]
     for m in range(mp_size):
@@ -1632,7 +1653,7 @@
     share = own_parts[0].shape[0] // 8 - quarter
     own_size = round_up(quarter + share, dp_size)
     split_size = round_up(quarter, dp_size)
-    conv_size = round_up(CONV_ROWS // 8, dp_size * mp_size)
+    conv_size = round_up((CONV_ROWS + FAST_ROWS) // 8, dp_size * mp_size)
     places, at = {}, 0
     for name, size in [("split", split_size), ("own", own_size), ("conv", conv_size)]:
         places[name] = at
@@ -1659,11 +1680,11 @@
     def tiled(size, *lead):
         return pltpu.VMEM((*lead, size, 8, 128), F32)
 
-    outs = [(EARLY_ROWS // 8, 8, 128), (share * mp_size, 8, 128), (quarter, 8, 128), (8, 128)]
+    outs = [(EARLY_ROWS // 8, 8, 128), (FAST_ROWS // 8, 8, 128), (share * mp_size, 8, 128), (quarter, 8, 128), (8, 128)]
     results = pl.pallas_call(
         partial(reduce_kernel, plan),
         in_specs=[any_spec] * loads,
-        out_specs=[any_spec, any_spec, any_spec, vmem],
+        out_specs=[any_spec] * 4 + [vmem],
         out_shape=[jax.ShapeDtypeStruct(shape, F32) for shape in outs],
         scratch_shapes=[
             tiled(quarter, mp_size),
@@ -1678,7 +1699,7 @@
             pltpu.SemaphoreType.DMA((loads,)),
             pltpu.SemaphoreType.DMA((copies,)),
             pltpu.SemaphoreType.DMA((copies,)),
-            pltpu.SemaphoreType.DMA((2 + 2 * mp_size,)),
+            pltpu.SemaphoreType.DMA((3 + 2 * mp_size,)),
         ],
         compiler_params=pltpu.CompilerParams(
             collective_id=1, has_side_effects=True, vmem_limit_bytes=62 * 1024 * 1024
@@ -1696,8 +1717,12 @@
 
 def adam_kernel(
     wins,
+    dp_size,
+    mp_size,
     early_ref,
-    rows_ref,
+    times_ref,
+    dense_ref,
+    table_ref,
     small_ref,
     split_ref,
     square_ref,
@@ -1715,12 +1740,13 @@
     split_new_first_ref,
     split_new_second_ref,
     split_low_ref,
-    scalar_ref,
+    norm_out,
+    loss_out,
+    count_out,
     split_in,
     split_out,
     field,
-    rows,
-    notes,
+    times,
     marks,
     pulled,
     factor_ref,
@@ -1730,6 +1756,7 @@
 ):
     step = pl.program_id(0)
     last = pl.num_programs(0) - 1
+    scalar_refs = (norm_out, loss_out, count_out)
     lane = lax.broadcasted_iota(jnp.int32, (1, 128), 1)
 
     def pull(block, slot):
@@ -1766,70 +1793,82 @@
     def prepare():
         for load in split_loads:
             load.start()
-        load_rows = pltpu.make_async_copy(rows_ref, rows, load_sem.at[0])
+        mark = pltpu.make_async_copy(table_ref, marks, load_sem.at[2])
+        mark.start()
+        load_times = pltpu.make_async_copy(
+            times_ref, times.at[pl.ds(0, FAST_ROWS)], load_sem.at[0]
+        )
+        load_times.start()
         load_early = pltpu.make_async_copy(
             early_ref, field.at[pl.ds(0, EARLY_ROWS)], load_sem.at[1]
         )
-        load_rows.start()
         load_early.start()
         late = FIELD_ROWS - EARLY_ROWS
         field[EARLY_ROWS:FIELD_ROWS] = jnp.zeros((late, 128), F32)
-        load_rows.wait()
-        stride = ROOM + 8
-        devices = rows.shape[0] // stride
-        notes[...] = rows[pl.ds(ROOM, devices, stride=stride), :]
-        mark = pltpu.make_async_copy(notes, marks, load_sem.at[2])
-        mark.start()
+        times[FAST_ROWS:] = jnp.zeros((times.shape[0] - FAST_ROWS, 128), F32)
+        lane_all = lax.broadcasted_iota(jnp.int32, table_ref.shape, 1)
+        counts = jnp.where(jnp.bitwise_and(lane_all, 2 * wins - 1) < wins, table_ref[...], 0.0)
+        count = sum_of(counts)
+        whole = jnp.sum(counts)
         mark.wait()
+        load_times.wait()
         place = lax.broadcasted_iota(jnp.int32, (SPAN, ROOM), 0)
         slot_of = lax.broadcasted_iota(jnp.int32, (SPAN, ROOM), 1)
 
-        def scatter(turn, carry):
+        def scatter(turn, begin):
             spots, found = [], []
-            for k in range(4):
-                device = turn * 4 + k
-                begin = jnp.int32(0)
+            for m in range(mp_size):
+                low = jnp.minimum(lax.div(begin, 8) * 8, FAST_ROWS)
                 picks = []
                 for w in range(wins):
-                    length = marks[device, w].astype(jnp.int32)
-                    row = marks[device, wins + w].astype(jnp.int32) + TABLE_AT
-                    low = lax.div(row, 8) * 8
-                    inside = (slot_of >= begin) & (slot_of < begin + length)
-                    inside = inside & (place - slot_of == row - low - begin)
+                    length = marks[turn, m * 2 * wins + w].astype(jnp.int32)
+                    row = marks[turn, m * 2 * wins + wins + w].astype(jnp.int32) + TABLE_AT
+                    base = lax.div(row, 8) * 8
+                    first = begin - low
+                    inside = (slot_of >= first) & (slot_of < first + length)
+                    inside = inside & (place - slot_of == row - base - first)
                     picks.append(jnp.where(inside, 1.0, 0.0).astype(BF16))
-                    spots.append(low)
+                    spots.append(base)
                     begin = begin + length
-                held = pair(rows[pl.ds(pl.multiple_of(device * stride, 8), ROOM)])
+                held = pair(times[pl.ds(pl.multiple_of(low, 8), ROOM)])
                 found.append(fold_pair(dot(jnp.concatenate(picks, axis=0), held)))
-            for k in range(4):
+            for m in range(mp_size):
                 for w in range(wins):
-                    spot = pl.ds(pl.multiple_of(spots[k * wins + w], 8), SPAN)
-                    field[spot] = field[spot] + found[k][w * SPAN : (w + 1) * SPAN]
-            return carry
-
-        lax.fori_loop(0, devices // 4, scatter, 0)
+                    spot = pl.ds(pl.multiple_of(spots[m * wins + w], 8), SPAN)
+                    field[spot] = field[spot] + found[m][w * SPAN : (w + 1) * SPAN]
+            return begin
+
+        @pl.when(whole <= FAST_ROWS)
+        def few():
+            lax.fori_loop(0, dp_size, scatter, jnp.int32(0))
+
+        @pl.when(whole > FAST_ROWS)
+        def many():
+            pull_dense = pltpu.make_async_copy(
+                dense_ref, field.at[pl.ds(EARLY_ROWS, late)], load_sem.at[0]
+            )
+            pull_dense.start()
+            pull_dense.wait()
 
         def fold(turn, carry):
-            spot = pl.multiple_of(EARLY_ROWS + turn * 64, 8)
-            held = field[pl.ds(spot, 64)]
-            return carry + jnp.sum((held * held).reshape(8, 8, 128), axis=0)
-
-        squares = lax.fori_loop(0, late // 64, fold, square_ref[...])
+            spot = pl.multiple_of(EARLY_ROWS + turn * 256, 8)
+            held = field[pl.ds(spot, 256)]
+            return carry + jnp.sum((held * held).reshape(32, 8, 128), axis=0)
+
+        squares = lax.fori_loop(0, late // 256, fold, square_ref[...])
         at = EARLY_ROWS
-        for name_at, count in [(0, 17), (24, ACT)]:
-            field[at : at + count] = small_ref[name_at : name_at + count]
-            at += count
+        for name_at, size in [(0, 17), (24, ACT)]:
+            field[at : at + size] = small_ref[name_at : name_at + size]
+            at += size
         at = TABLE_AT + TSTEPS
         field[at : at + ACT] = small_ref[48 : 48 + ACT]
-        lane_all = lax.broadcasted_iota(jnp.int32, notes.shape, 1)
-        count = sum_of(jnp.where(lane_all < wins, notes[...], 0.0))
         seed = 1.0 / count
         norm = jnp.sqrt(sum_of(squares)) * seed
         factor = jnp.minimum(1.0, clip_limit / (norm + 1e-06)) * seed
         factor_ref[...] = jnp.broadcast_to(factor, (8, 128))
         loss = small_ref[72:73]
-        row = lax.broadcasted_iota(jnp.int32, (8, 128), 0)
-        scalar_ref[...] = jnp.where(row == 0, norm, jnp.where(row == 1, loss, count))
+        for number, held in enumerate((norm, loss, count)):
+            scalar_refs[number][0] = jnp.sum(jnp.where(lane == 0, held, 0.0))
         load_early.wait()
         pull(0, 0).start()
 
@@ -1866,11 +1905,12 @@
     low_ref[...] = outs[0].astype(BF16)
 
 
-def adam_all(early, rows, small, split_grad, square, shared, split, wins):
+def adam_all(
+    early, times, dense, table, small, split_grad, square, shared, split, wins, dp_size, mp_size
+):
     grid = -(-FLAT_ROWS // BLOCK_ROWS)
     flat_spec = pl.BlockSpec((BLOCK_ROWS, 128), lambda i: (i, 0))
     split_rows = split[0].shape[0]
-    devices = rows.shape[0]
 
     def whole(shape):
         return pl.BlockSpec(shape, lambda i: (0,) * len(shape))
@@ -1879,11 +1919,13 @@
     split_out = jax.ShapeDtypeStruct((split_rows, 128), F32)
     any_spec = pl.BlockSpec(memory_space=pl.ANY)
     return pl.pallas_call(
-        partial(adam_kernel, wins),
+        partial(adam_kernel, wins, dp_size, mp_size),
         grid=(grid,),
         in_specs=[
             any_spec,
             any_spec,
+            any_spec,
+            pl.BlockSpec(memory_space=pltpu.VMEM),
             whole(small.shape),
             whole(split_grad.shape),
             whole((8, 128)),
@@ -1896,19 +1938,19 @@
         ],
         out_specs=[flat_spec] * 4
         + [any_spec] * 3
-        + [whole((split_rows, 128)), whole((8, 128))],
+        + [whole((split_rows, 128))]
+        + [pl.BlockSpec(memory_space=pltpu.SMEM)] * 3,
         out_shape=[shared_out] * 3
         + [jax.ShapeDtypeStruct((FLAT_ROWS, 128), BF16)]
         + [split_out] * 3
         + [jax.ShapeDtypeStruct((split_rows, 128), BF16)]
-        + [jax.ShapeDtypeStruct((8, 128), F32)],
+        + [jax.ShapeDtypeStruct((1,), F32)] * 3,
         scratch_shapes=[
             pltpu.VMEM((3, split_rows, 128), F32),
             pltpu.VMEM((3, split_rows, 128), F32),
             pltpu.VMEM((FIELD_ROWS, 128), F32),
-            pltpu.VMEM((devices * (ROOM + 8), 128), F32),
-            pltpu.VMEM((devices, 128), F32),
-            pltpu.SMEM((devices, 128), F32),
+            pltpu.VMEM((FAST_ROWS + ROOM, 128), F32),
+            pltpu.SMEM(table.shape, F32),
             pltpu.VMEM((2, BLOCK_ROWS + 8, 128), F32),
             pltpu.VMEM((8, 128), F32),
             pltpu.SemaphoreType.DMA((2,)),
@@ -1919,7 +1961,9 @@
         name="adam_update",
     )(
         early,
-        rows.reshape(devices * (ROOM + 8), 128),
+        times,
+        dense,
+        table,
         small,
         split_grad,
         square,
@@ -1950,8 +1994,24 @@
     packed = narrow == 32
     own_rows = split_weights.reshape(split_rows, 128)
     split_all = lax.all_gather(own_rows, "mp", axis=0)
+    notes = jnp.concatenate([lengths, starts]).astype(F32)
+    line = lax.dynamic_update_slice(
+        jnp.zeros((128,), F32), notes, (lax.axis_index("mp") * (2 * wins),)
+    )
+    here = jnp.arange(round_up(dp_size, 8)) == lax.axis_index("dp")
+    table = jnp.where(here[:, None], line[None, :], 0.0)
+    group = [table]
+    for k in range(1, mp_size):
+        turn = [(place, place ^ k) for place in range(mp_size)]
+        group.append(lax.ppermute(table, "mp", turn))
     flat = shared_weights.reshape(FLAT_ROWS, 128)
     picked, z_one, z_two, z_three = conv_forward(lengths, frames, flat)
+    z_three, group = lax.optimization_barrier((z_three, group))
+    table = sum(group[1:], group[0])
+    group = [table]
+    for k in range(1, dp_size):
+        turn = [(place, place ^ k) for place in range(dp_size)]
+        group.append(lax.ppermute(table, "dp", turn))
     if packed:
         weights = [split_all]
     else:
@@ -1969,12 +2029,14 @@
     cores, ys, xs, zs = mesh_bits(dp_size, mp_size)
     seat = jnp.bitwise_and(lax.axis_index("mp"), 1)
     seat = seat + 2 * jnp.bitwise_and(lax.axis_index("dp"), (1 << len(xs)) - 1)
-    index = jnp.stack([lax.axis_index("mp"), seat])
+    row, column = lax.axis_index("dp"), lax.axis_index("mp")
+    index = jnp.stack([column, seat, row])
     results = former(
         lengths, starts, index, returns, actions, z_three, flat, weights, small_rows, packed
     )
     d_three, rows = results[:2]
-    rows_all = lax.all_gather(rows, ("dp", "mp"), axis=0)
+    rows, group = lax.optimization_barrier((rows, group))
+    table = sum(group[1:], group[0])
     quarter = 3136 // mp_size
     if packed:
         split_parts, own_parts = results[2:6], results[6:]
@@ -2013,19 +2075,46 @@
             for mp in range(mp_size)
         ]
         own_parts[k] = lax.ppermute(own_parts[k], ("dp", "mp"), turn)
-    d_conv = conv_backward(lengths, picked, z_one, z_two, d_three, flat)
-    early, small, split_sum, square = reduce_all(
+    d_conv, total = conv_backward(
+        lengths, index, table, rows, picked, z_one, z_two, d_three, flat
+    )
+
+    def whole():
+        ends = jnp.cumsum(lengths)
+        slot = jnp.arange(ROOM, dtype=jnp.int32)
+        past = slot[:, None] >= ends[None, :-1]
+        begin = jnp.sum(jnp.where(past, lengths[None, :-1], 0), axis=1)
+        gaps = starts[1:] - starts[:-1]
+        spot = slot - begin + starts[0] + jnp.sum(jnp.where(past, gaps[None, :], 0), axis=1)
+        spot = jnp.where(slot < ends[-1], spot, 0) + TABLE_AT - EARLY_ROWS
+        held = jnp.zeros((FIELD_ROWS - EARLY_ROWS, D), F32).at[spot].add(rows)
+        return lax.psum(held, ("dp", "mp"))
+
+    dense = lax.cond(
+        total[0] > FAST_ROWS, whole, lambda: jnp.zeros((FIELD_ROWS - EARLY_ROWS, D), F32)
+    )
+    early, times, small, split_sum, square = reduce_all(
         split_parts, own_parts, d_conv, dp_size, mp_size
     )
     shared_view = [a.reshape(FLAT_ROWS, 128) for a in (shared_weights, shared_first, shared_second)]
     split_view = [a.reshape(split_rows, 128) for a in (split_weights, split_first, split_second)]
     updated = adam_all(
-        early, rows_all, small, split_sum, square, shared_view, split_view, wins
+        early,
+        times,
+        dense,
+        table,
+        small,
+        split_sum,
+        square,
+        shared_view,
+        split_view,
+        wins,
+        dp_size,
+        mp_size,
     )
     shared_out = [a.reshape(-1) for a in updated[:4]]
     split_out = [a.reshape(-1) for a in updated[4:8]]
-    scalars = updated[8]
-    return (*shared_out, *split_out, scalars[0, 0], scalars[1, 0], scalars[2, 0])
+    return (*shared_out, *split_out, *[held.reshape(()) for held in updated[8:]])
 
 
 def solution(mesh):

time: 185 us -> 203 us (1.097)
  starting transfers between devices: 4.14 us -> 19.3 us
    ppermute x0 -> x10, starting transfers between devices: none -> 14.1 us  [the longest x7 10.9 us: per_device(): group.append(lax.ppermute(table, 'dp', turn))]
    ppermute x0 -> x10, waiting for transfers between devices: none -> 10.5 us  [the longest x7 10.5 us: per_device(): group.append(lax.ppermute(table, 'dp', turn))]
    ppermute x3, waiting for transfers between devices: 6.33 us -> 0.01 us  [per_device(): split_parts[k] = lax.ppermute(split_parts[k], 'mp', turn)]
    all_gather x1, waiting for transfers between devices: 14.6 us -> 10.5 us  [per_device(): split_all = lax.all_gather(own_rows, 'mp', axis=0)]
  transfers between devices with their start and end apart: 8 -> 17, of which waited for: 2 -> 5; matrix products, arithmetic and copies ran while one was open for 0% -> 2% of each run, Pallas kernels for 48% -> 11%
where the time goes in v1:
time: 203 us; the launch traced here: 202 us
  Pallas kernels  141 us (69%)
  waiting for transfers between devices  21.8 us (11%)
  starting transfers between devices  19.3 us (10%)
  between operations  14.9 us (7%)
  local copies, waits for them, and re-layouts  2.56 us (1%)
  other arithmetic  2.17 us (1%)
    pallas_call x1, Pallas kernels, reduce_all(): pl.pallas_call(partial(reduce_kernel, plan), in_specs=[any_spec] * loads,...  67.6 us
    pallas_call x1, Pallas kernels, former(): pl.pallas_call(partial(former_kernel, packed), in_specs=[hbm] * 3 + [vmem...  31.8 us
    pallas_call x1, Pallas kernels, adam_all(): pl.pallas_call(partial(adam_kernel, wins, dp_size, mp_size), grid=(grid,)...  18.8 us
    pallas_call x1, Pallas kernels, conv_backward(): pl.pallas_call(conv_backward_kernel, in_specs=[hbm] * 2 + [vmem] * 2 + [h...  14 us
    ppermute x7, starting transfers between devices, per_device(): group.append(lax.ppermute(table, 'dp', turn))  10.9 us
    all_gather x1, waiting for transfers between devices, per_device(): split_all = lax.all_gather(own_rows, 'mp', axis=0)  10.5 us
    ppermute x7, waiting for transfers between devices, per_device(): group.append(lax.ppermute(table, 'dp', turn))  10.5 us
    pallas_call x1, Pallas kernels, conv_forward(): pl.pallas_call(conv_forward_kernel, in_specs=[any_spec, any_spec, any_spe...  8.98 us
  transfers between devices with their start and end apart: 17, of which 5 were waited for; matrix products, arithmetic and copies ran while one was open for 2% of the time, Pallas kernels for 11%

profile of v1, /device:TPU:0, one launch (start us, length us, event | category | flops | bytes accessed | tf_op | source)
XLA Modules:
  0.0 201.9 jit_solution(6763425697318020053)
XLA Ops:
  7.2 0.0 all-gather.2.cloned.1.call-start
  7.2 0.7 all-gather.2.cloned.1.call-update
  7.9 0.8 fusion.4
  8.8 0.1 broadcast_select_fusion
  8.9 0.5 collective-permute-start
  9.3 2.6 %collective-permute-start.1 = (f32[8,128]{1,0:T(8,128)S(1)}, f32[8,128]{1,0:T(8,128)S(1)}, u32[]{:S(2)}, u32[]{:S(2)}) collective-permute-start(f32[8,128]{1,0:T(8,128)S(1)} %broadcast_select_fusion), channel_id=1, source_target_pairs={{0,2},{1,3},{2,0},{3,1},{4,6},{5,7},{6,4},{7,5},{8,10},{9,11},{10,... | collective-permute-start | bytes 12296 | tf_op jit(solution)/shard_map/ppermute | solution.py:2006
  11.9 0.1 collective-permute-start.2
  12.0 0.6 pad_add_fusion.index_from
  12.6 9.0 %conv_forward.1 = (bf16[8,21,4,16,640]{4,3,2,1,0:T(8,128)(2,1)}, f32[8,10,2,5,16,128]{5,4,3,2,1,0:T(8,128)}, f32[8,9,5,16,128]{4,3,2,1,0:T(8,128)}, f32[28,128,128]{2,1,0:T(8,128)}) custom-call(s32[4]{0:T(128)} %lengths_from.5, bf16[4,30,84,4,84]{4,3,2,1,0:T(4,128)(2,1)} %bitcast.63, f32[7896,128]{1,0:T(8,128)} %bitcast.59), custom_call_target="tpu_custom_call" | custom-call | tf_op jit(solution)/shard_map/conv_forward/pallas_call | solution.py:367
  21.6 0.0 collective-permute-done
  21.6 0.0 collective-permute-done.1
  21.6 0.0 collective-permute-done.2
  21.6 10.5 %all-gather.2.cloned.1.call-done.refs_0_ = f32[4,770,128]{2,1,0:T(8,128)} async-done(((f32[1,770,128]{2,1,0:T(8,128)}), f32[4,770,128]{2,1,0:T(8,128)}) %all-gather.2.cloned.1.call-update) | async-done | bytes 1576976 | tf_op jit(solution)/shard_map/all_gather | solution.py:1996
  32.1 31.8 %transformer_step.1 = (f32[28,128,128]{2,1,0:T(8,128)}, f32[128,128]{1,0:T(8,128)S(1)}, f32[784,128]{1,0:T(8,128)}, f32[784,128]{1,0:T(8,128)}, f32[784,128]{1,0...) custom-call(s32[4]{0:T(128)S(1)} %copy-done.4, ...), custom_call_target="tpu_custom_call" | custom-call | tf_op jit(solution)/shard_map/transformer_step/pallas_call | solution.py:1330
  64.0 0.3 collective-permute-start.3
  64.3 1.5 collective-permute-start.9
  65.7 1.5 collective-permute-start.10
  67.2 0.5 collective-permute-start.11
  67.8 2.4 %collective-permute-start.12 = (f32[8,128]{1,0:T(8,128)S(1)}, f32[8,128]{1,0:T(8,128)S(1)}, u32[]{:S(2)}, u32[]{:S(2)}) collective-permute-start(f32[8,128]{1,0:T(8,128)S(1)} %add_add_fusion.1), channel_id=1, source_target_pairs={{0,16},{4,20},{8,24},{12,28},{16,0},{20,4},{24,8},{28,12},{1,17},{... | collective-permute-start | bytes 12296 | tf_op jit(solution)/shard_map/ppermute | solution.py:2014
  70.2 0.0 collective-permute-done.9
  70.2 1.4 collective-permute-start.13
  71.6 0.0 collective-permute-done.10
  71.6 0.0 collective-permute-start.6
  71.6 0.1 collective-permute-done.11
  71.7 0.6 collective-permute-start.7
  72.3 0.0 collective-permute-done.12
  72.3 1.2 collective-permute-start.8
  73.5 2.2 %collective-permute-done.13 = f32[8,128]{1,0:T(8,128)S(1)} collective-permute-done((f32[8,128]{1,0:T(8,128)S(1)}, f32[8,128]{1,0:T(8,128)S(1)}, u32[]{:S(2)}, u32[]{:S(2)}) %collective-permute-start.13) | collective-permute-done | bytes 4128 | tf_op jit(solution)/shard_map/ppermute | solution.py:2014
  75.7 1.4 collective-permute-start.14
  77.0 4.0 %collective-permute-done.14 = f32[8,128]{1,0:T(8,128)S(1)} collective-permute-done((f32[8,128]{1,0:T(8,128)S(1)}, f32[8,128]{1,0:T(8,128)S(1)}, u32[]{:S(2)}, u32[]{:S(2)}) %collective-permute-start.14) | collective-permute-done | bytes 4128 | tf_op jit(solution)/shard_map/ppermute | solution.py:2014
  81.1 2.3 %collective-permute-start.15 = (f32[8,128]{1,0:T(8,128)S(1)}, f32[8,128]{1,0:T(8,128)S(1)}, u32[]{:S(2)}, u32[]{:S(2)}) collective-permute-start(f32[8,128]{1,0:T(8,128)S(1)} %add_add_fusion.1), channel_id=1, source_target_pairs={{0,28},{4,24},{8,20},{12,16},{16,12},{20,8},{24,4},{28,0},{1,29},{... | collective-permute-start | bytes 12296 | tf_op jit(solution)/shard_map/ppermute | solution.py:2014
  83.4 4.1 %collective-permute-done.15 = f32[8,128]{1,0:T(8,128)S(1)} collective-permute-done((f32[8,128]{1,0:T(8,128)S(1)}, f32[8,128]{1,0:T(8,128)S(1)}, u32[]{:S(2)}, u32[]{:S(2)}) %collective-permute-start.15) | collective-permute-done | bytes 4128 | tf_op jit(solution)/shard_map/ppermute | solution.py:2014
  87.5 3.2 %collective-permute-start.4 = (f32[784,128]{1,0:T(8,128)}, f32[784,128]{1,0:T(8,128)}, u32[]{:S(2)}, u32[]{:S(2)}) collective-permute-start(f32[784,128]{1,0:T(8,128)} %get-tuple-element.73), channel_id=1, source_target_pairs={{0,2},{1,3},{2,0},{3,1},{4,6},{5,7},{6,4},{7,5},{8,10},{9,11},{10,... | collective-permute-start | bytes 1204232 | tf_op jit(solution)/shard_map/ppermute | solution.py:2071
  90.7 0.0 collective-permute-done.3
  90.7 0.0 collective-permute-start.5
  90.7 0.7 add_add_fusion.table_ref
  91.3 14.0 %conv_backward.1 = (f32[1384,128]{1,0:T(8,128)}, s32[1]{0:T(128)}) custom-call(s32[4]{0:T(128)S(1)} %copy-done.4, s32[3]{0:T(128)} %pad_add_fusion.index_from, f32[8,128]{1,0:T(8,128)} %add_add_fusion.table_ref, f32[128,128]{1,0:T(8,128)S(1)} %get-tuple-element.92.times_ref, bf16[8,21,4,16,640]{4,3,2,1,0:T(8,128)(2,1)} %get-tuple-element.93.picked_ref, ...), custom_call_target="tpu_custom_call" | custom-call | tf_op jit(solution)/shard_map/conv_backward/pallas_call | solution.py:694
  106.0 1.6 conditional.1
  106.0 1.6 broadcast.63
  107.6 0.0 collective-permute-done.4
  107.6 0.0 copy-start
  107.6 0.0 collective-permute-done.7
  107.6 0.0 copy-start.1
  107.6 0.7 copy-done
  108.3 0.1 copy-done.1
  108.5 0.1 copy-done.2
  108.6 67.6 %reduce_gradients.1 = (f32[469,8,128]{2,1,0:T(8,128)}, f32[96,8,128]{2,1,0:T(8,128)}, f32[12,8,128]{2,1,0:T(8,128)}, f32[98,8,128]{2,1,0:T(8,128)}, f32[8,128]{1,0:T(8,128)}) custom-call(f32[98,8,128]{2,1,0:T(8,128)} %bitcast.74, f32[98,8,128]{2,1,0:T(8,128)} %bitcast.75, f32[98,8,128]{2,1,0:T(8,128)} %bitcast.15.refs_2_, f32[98,8,128]{2,1,0:T(8,128)} %bitcast.16.refs_3_, ...), custom_call_target="tpu_custom_call" | custom-call | tf_op jit(solution)/shard_map/reduce_gradients/pallas_call | solution.py:1684
  176.2 18.8 %adam_update.1 = (f32[7896,128]{1,0:T(8,128)}, f32[7896,128]{1,0:T(8,128)}, f32[7896,128]{1,0:T(8,128)}, bf16[7896,128]{1,0:T(8,128)(2,1)}, f32[770,128]{1,0:T(8...) custom-call(f32[3752,128]{1,0:T(8,128)} %bitcast.66, ...), custom_call_target="tpu_custom_call" | custom-call | tf_op jit(solution)/shard_map/adam_update/pallas_call | solution.py:1921
  (13 shorter events, 0.0 us)
Async XLA Ops:
  7.2 25.0 %all-gather.2.cloned.1.call-start = ((), (), s32[]{:S(2)}) async-start(), calls=%async_computation.1 | async-start | bytes 1986560 | tf_op jit(solution)/shard_map/all_gather | solution.py:1996
  8.9 12.7 %collective-permute-start = (f32[8,128]{1,0:T(8,128)S(1)}, f32[8,128]{1,0:T(8,128)S(1)}, u32[]{:S(2)}, u32[]{:S(2)}) collective-permute-start(f32[8,128]{1,0:T(8,128)S(1)} %broadcast_select_fusion), channel_id=1, source_target_pairs={{0,1},{1,0},{2,3},{3,2},{4,5},{5,4},{6,7},{7,6},{8,9},{9,8},{10,11... | collective-permute-start | bytes 12296 | tf_op jit(solution)/shard_map/ppermute | solution.py:2006
  9.3 12.3 %collective-permute-start.1 = (f32[8,128]{1,0:T(8,128)S(1)}, f32[8,128]{1,0:T(8,128)S(1)}, u32[]{:S(2)}, u32[]{:S(2)}) collective-permute-start(f32[8,128]{1,0:T(8,128)S(1)} %broadcast_select_fusion), channel_id=1, source_target_pairs={{0,2},{1,3},{2,0},{3,1},{4,6},{5,7},{6,4},{7,5},{8,10},{9,11},{10,... | collective-permute-start | bytes 12296 | tf_op jit(solution)/shard_map/ppermute | solution.py:2006
  11.9 9.7 %collective-permute-start.2 = (f32[8,128]{1,0:T(8,128)S(1)}, f32[8,128]{1,0:T(8,128)S(1)}, u32[]{:S(2)}, u32[]{:S(2)}) collective-permute-start(f32[8,128]{1,0:T(8,128)S(1)} %broadcast_select_fusion), channel_id=1, source_target_pairs={{0,3},{1,2},{2,1},{3,0},{4,7},{5,6},{6,5},{7,4},{8,11},{9,10},{10,... | collective-permute-start | bytes 12296 | tf_op jit(solution)/shard_map/ppermute | solution.py:2006
  12.6 19.6 %copy-start.4 = (s32[4]{0:T(128)S(1)}, s32[4]{0:T(128)}, u32[]{:S(2)}) copy-start(s32[4]{0:T(128)} %lengths_from.5) | copy-start | bytes 52
  12.6 19.6 %copy-start.5 = (s32[4]{0:T(128)S(1)}, s32[4]{0:T(128)}, u32[]{:S(2)}) copy-start(s32[4]{0:T(128)} %starts_from.1) | copy-start | bytes 52
  64.0 26.7 %collective-permute-start.3 = (f32[784,128]{1,0:T(8,128)}, f32[784,128]{1,0:T(8,128)S(1)}, u32[]{:S(2)}, u32[]{:S(2)}) collective-permute-start(f32[784,128]{1,0:T(8,128)} %get-tuple-element.72), channel_id=1, source_target_pairs={{0,1},{1,0},{2,3},{3,2},{4,5},{5,4},{6,7},{7,6},{8,9},{9,8},{10,11... | collective-permute-start | bytes 1204232 | tf_op jit(solution)/shard_map/ppermute | solution.py:2071
  64.3 5.9 %collective-permute-start.9 = (f32[8,128]{1,0:T(8,128)S(1)}, f32[8,128]{1,0:T(8,128)S(1)}, u32[]{:S(2)}, u32[]{:S(2)}) collective-permute-start(f32[8,128]{1,0:T(8,128)S(1)} %add_add_fusion.1), channel_id=1, source_target_pairs={{0,4},{4,0},{8,12},{12,8},{16,20},{20,16},{24,28},{28,24},{1,5},{5... | collective-permute-start | bytes 12296 | tf_op jit(solution)/shard_map/ppermute | solution.py:2014
  65.7 5.9 %collective-permute-start.10 = (f32[8,128]{1,0:T(8,128)S(1)}, f32[8,128]{1,0:T(8,128)S(1)}, u32[]{:S(2)}, u32[]{:S(2)}) collective-permute-start(f32[8,128]{1,0:T(8,128)S(1)} %add_add_fusion.1), channel_id=1, source_target_pairs={{0,8},{4,12},{8,0},{12,4},{16,24},{20,28},{24,16},{28,20},{1,9},{5... | collective-permute-start | bytes 12296 | tf_op jit(solution)/shard_map/ppermute | solution.py:2014
  67.2 4.5 %collective-permute-start.11 = (f32[8,128]{1,0:T(8,128)S(1)}, f32[8,128]{1,0:T(8,128)S(1)}, u32[]{:S(2)}, u32[]{:S(2)}) collective-permute-start(f32[8,128]{1,0:T(8,128)S(1)} %add_add_fusion.1), channel_id=1, source_target_pairs={{0,12},{4,8},{8,4},{12,0},{16,28},{20,24},{24,20},{28,16},{1,13},{... | collective-permute-start | bytes 12296 | tf_op jit(solution)/shard_map/ppermute | solution.py:2014
  67.8 4.6 %collective-permute-start.12 = (f32[8,128]{1,0:T(8,128)S(1)}, f32[8,128]{1,0:T(8,128)S(1)}, u32[]{:S(2)}, u32[]{:S(2)}) collective-permute-start(f32[8,128]{1,0:T(8,128)S(1)} %add_add_fusion.1), channel_id=1, source_target_pairs={{0,16},{4,20},{8,24},{12,28},{16,0},{20,4},{24,8},{28,12},{1,17},{... | collective-permute-start | bytes 12296 | tf_op jit(solution)/shard_map/ppermute | solution.py:2014
  70.2 5.5 %collective-permute-start.13 = (f32[8,128]{1,0:T(8,128)S(1)}, f32[8,128]{1,0:T(8,128)S(1)}, u32[]{:S(2)}, u32[]{:S(2)}) collective-permute-start(f32[8,128]{1,0:T(8,128)S(1)} %add_add_fusion.1), channel_id=1, source_target_pairs={{0,20},{4,16},{8,28},{12,24},{16,4},{20,0},{24,12},{28,8},{1,21},{... | collective-permute-start | bytes 12296 | tf_op jit(solution)/shard_map/ppermute | solution.py:2014
  71.6 36.0 %collective-permute-start.6 = (f32[808,128]{1,0:T(8,128)}, f32[808,128]{1,0:T(8,128)S(1)}, u32[]{:S(2)}, u32[]{:S(2)}) collective-permute-start(f32[808,128]{1,0:T(8,128)} %get-tuple-element.76), channel_id=1, source_target_pairs={{0,1},{1,0},{2,3},{3,2},{4,5},{5,4},{6,7},{7,6},{8,9},{9,8},{10,11... | collective-permute-start | bytes 1241096 | tf_op jit(solution)/shard_map/ppermute | solution.py:2077
  71.7 35.9 %collective-permute-start.7 = (f32[808,128]{1,0:T(8,128)}, f32[808,128]{1,0:T(8,128)S(1)}, u32[]{:S(2)}, u32[]{:S(2)}) collective-permute-start(f32[808,128]{1,0:T(8,128)} %get-tuple-element.77), channel_id=1, source_target_pairs={{0,4},{1,5},{2,6},{3,7},{4,0},{5,1},{6,2},{7,3},{8,12},{9,13},{10,... | collective-permute-start | bytes 1241096 | tf_op jit(solution)/shard_map/ppermute | solution.py:2077
  72.3 35.3 %collective-permute-start.8 = (f32[808,128]{1,0:T(8,128)}, f32[808,128]{1,0:T(8,128)S(1)}, u32[]{:S(2)}, u32[]{:S(2)}) collective-permute-start(f32[808,128]{1,0:T(8,128)} %get-tuple-element.78), channel_id=1, source_target_pairs={{0,5},{1,4},{2,7},{3,6},{4,1},{5,0},{6,3},{7,2},{8,13},{9,12},{10,... | collective-permute-start | bytes 1241096 | tf_op jit(solution)/shard_map/ppermute | solution.py:2077
  75.7 5.4 %collective-permute-start.14 = (f32[8,128]{1,0:T(8,128)S(1)}, f32[8,128]{1,0:T(8,128)S(1)}, u32[]{:S(2)}, u32[]{:S(2)}) collective-permute-start(f32[8,128]{1,0:T(8,128)S(1)} %add_add_fusion.1), channel_id=1, source_target_pairs={{0,24},{4,28},{8,16},{12,20},{16,8},{20,12},{24,0},{28,4},{1,25},{... | collective-permute-start | bytes 12296 | tf_op jit(solution)/shard_map/ppermute | solution.py:2014
  81.1 6.4 %collective-permute-start.15 = (f32[8,128]{1,0:T(8,128)S(1)}, f32[8,128]{1,0:T(8,128)S(1)}, u32[]{:S(2)}, u32[]{:S(2)}) collective-permute-start(f32[8,128]{1,0:T(8,128)S(1)} %add_add_fusion.1), channel_id=1, source_target_pairs={{0,28},{4,24},{8,20},{12,16},{16,12},{20,8},{24,4},{28,0},{1,29},{... | collective-permute-start | bytes 12296 | tf_op jit(solution)/shard_map/ppermute | solution.py:2014
  87.5 20.1 %collective-permute-start.4 = (f32[784,128]{1,0:T(8,128)}, f32[784,128]{1,0:T(8,128)}, u32[]{:S(2)}, u32[]{:S(2)}) collective-permute-start(f32[784,128]{1,0:T(8,128)} %get-tuple-element.73), channel_id=1, source_target_pairs={{0,2},{1,3},{2,0},{3,1},{4,6},{5,7},{6,4},{7,5},{8,10},{9,11},{10,... | collective-permute-start | bytes 1204232 | tf_op jit(solution)/shard_map/ppermute | solution.py:2071
  90.7 14.7 %copy-start.3 = (f32[784,128]{1,0:T(8,128)}, f32[784,128]{1,0:T(8,128)S(1)}, u32[]{:S(2)}) copy-start(f32[784,128]{1,0:T(8,128)S(1)} %collective-permute-done.3) | copy-start | bytes 1204228
  90.7 16.9 %collective-permute-start.5 = (f32[784,128]{1,0:T(8,128)}, f32[784,128]{1,0:T(8,128)}, u32[]{:S(2)}, u32[]{:S(2)}) collective-permute-start(f32[784,128]{1,0:T(8,128)} %get-tuple-element.74), channel_id=1, source_target_pairs={{0,3},{1,2},{2,1},{3,0},{4,7},{5,6},{6,5},{7,4},{8,11},{9,10},{10,... | collective-permute-start | bytes 1204232 | tf_op jit(solution)/shard_map/ppermute | solution.py:2071
  107.6 0.8 copy-start
  107.6 0.9 copy-start.1
  107.6 1.0 copy-start.2
Sparse Core Ops, SparseCore 0:
  9.6 22.4 all-gather.1

commit v2 on v0

--- a/solution.py
+++ b/solution.py
@@ -1085,6 +1085,7 @@
 
 def former_kernel(
     packed,
+    slots,
     lengths_from,
     starts_from,
     index_from,
@@ -1156,14 +1157,7 @@
     for copy in copies:
         copy.start()
 
-    @pl.when(used <= HALF)
-    def few_states():
-        z_copy(HALF).start()
-
-    @pl.when(used > HALF)
-    def many_states():
-        z_copy(ROOM).start()
-
+    z_copy(slots).start()
     if packed:
         unpack_split(split_ref, *weights)
     for copy in copies:
@@ -1209,39 +1203,30 @@
     rows_ref[ROOM : ROOM + 1] = note
     d_small_ref[...] = jnp.zeros(d_small_ref.shape, F32)
 
-    def run(slots):
-        z_copy(slots).wait()
-        former_body(
-            slots,
-            used,
-            lengths_ref,
-            returns_ref,
-            actions_ref,
-            head_ref,
-            z_ref,
-            small,
-            times_all,
-            encoder,
-            weights,
-            d_three_ref,
-            d_encoder_ref,
-            d_small_ref,
-            rows_ref,
-            grads,
-            chances,
-            kept,
-            sums,
-            flats,
-        )
-        z_back(slots).start()
-
-    @pl.when(used <= HALF)
-    def few():
-        run(HALF)
-
-    @pl.when(used > HALF)
-    def many():
-        run(ROOM)
+    z_copy(slots).wait()
+    former_body(
+        slots,
+        used,
+        lengths_ref,
+        returns_ref,
+        actions_ref,
+        head_ref,
+        z_ref,
+        small,
+        times_all,
+        encoder,
+        weights,
+        d_three_ref,
+        d_encoder_ref,
+        d_small_ref,
+        rows_ref,
+        grads,
+        chances,
+        kept,
+        sums,
+        flats,
+    )
+    z_back(slots).start()
 
     if packed:
         count = d_small_ref.shape[0] // 4
@@ -1254,16 +1239,12 @@
             held = d_small_ref[pl.ds(pl.multiple_of(e * count, 8), count)]
             parts[4 + k][784 : 784 + count] = held
 
-    @pl.when(used <= HALF)
-    def few_end():
-        z_back(HALF).wait()
-
-    @pl.when(used > HALF)
-    def many_end():
-        z_back(ROOM).wait()
-
-
-def former(lengths, starts, index, returns, actions, z_three, flat, weights, small_rows, packed):
+    z_back(slots).wait()
+
+
+def former(
+    lengths, starts, index, returns, actions, z_three, flat, weights, small_rows, packed, slots
+):
     vmem = pl.BlockSpec(memory_space=pltpu.VMEM)
     hbm = pl.BlockSpec(memory_space=pltpu.HBM)
     wins = lengths.shape[0]
@@ -1288,7 +1269,7 @@
         outs += [(3136, 128), (small_rows, 128)] + canonical
         out_specs += [vmem] * 7
         scratch = []
-    rows = 3 * ROOM
+    rows = 3 * slots
     scratch += [
         pltpu.VMEM((3144, 128), F32),
         pltpu.VMEM((3136, 128), F32),
@@ -1309,13 +1290,13 @@
         pltpu.SemaphoreType.DMA((wins + 7,)),
     ]
     return pl.pallas_call(
-        partial(former_kernel, packed),
+        partial(former_kernel, packed, slots),
         in_specs=[hbm] * 3 + [vmem] * 2 + [hbm] * 2 + [vmem] * len(weights),
         out_specs=out_specs,
         out_shape=[jax.ShapeDtypeStruct(shape, F32) for shape in outs],
         scratch_shapes=scratch,
         compiler_params=pltpu.CompilerParams(vmem_limit_bytes=62 * 1024 * 1024),
-        name="transformer_step",
+        name=f"transformer_step_{slots}",
     )(lengths, starts, index, returns, actions, z_three, flat, *weights)
 
 
@@ -1715,7 +1696,9 @@
     split_new_first_ref,
     split_new_second_ref,
     split_low_ref,
-    scalar_ref,
+    norm_out,
+    loss_out,
+    count_out,
     split_in,
     split_out,
     field,
@@ -1730,6 +1713,7 @@
 ):
     step = pl.program_id(0)
     last = pl.num_programs(0) - 1
+    scalar_refs = (norm_out, loss_out, count_out)
     lane = lax.broadcasted_iota(jnp.int32, (1, 128), 1)
 
     def pull(block, slot):
@@ -1810,15 +1794,15 @@
         lax.fori_loop(0, devices // 4, scatter, 0)
 
         def fold(turn, carry):
-            spot = pl.multiple_of(EARLY_ROWS + turn * 64, 8)
-            held = field[pl.ds(spot, 64)]
-            return carry + jnp.sum((held * held).reshape(8, 8, 128), axis=0)
-
-        squares = lax.fori_loop(0, late // 64, fold, square_ref[...])
+            spot = pl.multiple_of(EARLY_ROWS + turn * 256, 8)
+            held = field[pl.ds(spot, 256)]
+            return carry + jnp.sum((held * held).reshape(32, 8, 128), axis=0)
+
+        squares = lax.fori_loop(0, late // 256, fold, square_ref[...])
         at = EARLY_ROWS
-        for name_at, count in [(0, 17), (24, ACT)]:
-            field[at : at + count] = small_ref[name_at : name_at + count]
-            at += count
+        for name_at, size in [(0, 17), (24, ACT)]:
+            field[at : at + size] = small_ref[name_at : name_at + size]
+            at += size
         at = TABLE_AT + TSTEPS
         field[at : at + ACT] = small_ref[48 : 48 + ACT]
         lane_all = lax.broadcasted_iota(jnp.int32, notes.shape, 1)
@@ -1828,8 +1812,8 @@
         factor = jnp.minimum(1.0, clip_limit / (norm + 1e-06)) * seed
         factor_ref[...] = jnp.broadcast_to(factor, (8, 128))
         loss = small_ref[72:73]
-        row = lax.broadcasted_iota(jnp.int32, (8, 128), 0)
-        scalar_ref[...] = jnp.where(row == 0, norm, jnp.where(row == 1, loss, count))
+        for number, held in enumerate((norm, loss, count)):
+            scalar_refs[number][0] = jnp.sum(jnp.where(lane == 0, held, 0.0))
         load_early.wait()
         pull(0, 0).start()
 
@@ -1896,12 +1880,13 @@
         ],
         out_specs=[flat_spec] * 4
         + [any_spec] * 3
-        + [whole((split_rows, 128)), whole((8, 128))],
+        + [whole((split_rows, 128))]
+        + [pl.BlockSpec(memory_space=pltpu.SMEM)] * 3,
         out_shape=[shared_out] * 3
         + [jax.ShapeDtypeStruct((FLAT_ROWS, 128), BF16)]
         + [split_out] * 3
         + [jax.ShapeDtypeStruct((split_rows, 128), BF16)]
-        + [jax.ShapeDtypeStruct((8, 128), F32)],
+        + [jax.ShapeDtypeStruct((1,), F32)] * 3,
         scratch_shapes=[
             pltpu.VMEM((3, split_rows, 128), F32),
             pltpu.VMEM((3, split_rows, 128), F32),
@@ -1970,8 +1955,17 @@
     seat = jnp.bitwise_and(lax.axis_index("mp"), 1)
     seat = seat + 2 * jnp.bitwise_and(lax.axis_index("dp"), (1 << len(xs)) - 1)
     index = jnp.stack([lax.axis_index("mp"), seat])
-    results = former(
-        lengths, starts, index, returns, actions, z_three, flat, weights, small_rows, packed
+    def step_of(slots):
+        def run(operands):
+            return tuple(former(*operands, small_rows, packed, slots))
+
+        return run
+
+    results = lax.cond(
+        jnp.sum(lengths) <= HALF,
+        step_of(HALF),
+        step_of(ROOM),
+        (lengths, starts, index, returns, actions, z_three, flat, weights),
     )
     d_three, rows = results[:2]
     rows_all = lax.all_gather(rows, ("dp", "mp"), axis=0)
@@ -2024,8 +2018,7 @@
     )
     shared_out = [a.reshape(-1) for a in updated[:4]]
     split_out = [a.reshape(-1) for a in updated[4:8]]
-    scalars = updated[8]
-    return (*shared_out, *split_out, scalars[0, 0], scalars[1, 0], scalars[2, 0])
+    return (*shared_out, *split_out, *[held.reshape(()) for held in updated[8:]])
 
 
 def solution(mesh):

time: 185 us -> 205 us (1.11)
  the two profiles are of different devices: /device:TPU:0 before, /device:TPU:19 now
where the time goes in v2:
time: 205 us; the launch traced here: 201 us
  Pallas kernels  145 us (71%)
  between operations  15.4 us (8%)
  starting transfers between devices  14 us (7%)
  waiting for transfers between devices  13.3 us (6%)
  loops' own time  11.1 us (5%)
    pallas_call x1, Pallas kernels, reduce_all(): pl.pallas_call(partial(reduce_kernel, plan), in_specs=[any_spec] * loads,...  73 us
    pallas_call x1, Pallas kernels, former(): pl.pallas_call(partial(former_kernel, packed, slots), in_specs=[hbm] * 3...  30.7 us
    pallas_call x1, Pallas kernels, adam_all(): pl.pallas_call(partial(adam_kernel, wins), grid=(grid,), in_specs=[any_sp...  20.1 us
    pallas_call x1, Pallas kernels, conv_backward(): pl.pallas_call(conv_backward_kernel, in_specs=[hbm] * 6, out_specs=vmem,...  12.5 us
    all_gather x1, waiting for transfers between devices, per_device(): split_all = lax.all_gather(own_rows, 'mp', axis=0)  12.1 us
    another operation x1, loops' own time, per_device(): lax.cond(jnp.sum(lengths) <= HALF, step_of(HALF), step_of(ROOM), (lengths...  11.1 us
    pallas_call x1, Pallas kernels, conv_forward(): pl.pallas_call(conv_forward_kernel, in_specs=[any_spec, any_spec, any_spe...  8.68 us
    ppermute x3, starting transfers between devices, per_device(): own_parts[k] = lax.ppermute(own_parts[k], ('dp', 'mp'), turn)  6.99 us
  transfers between devices with their start and end apart: 8, of which 2 were waited for; matrix products, arithmetic and copies ran while one was open for 1% of the time, Pallas kernels for 47%

profile of v2, /device:TPU:19, one launch (start us, length us, event | category | flops | bytes accessed | tf_op | source)
XLA Modules:
  0.0 201.1 jit_solution(16971158177188448535)
XLA Ops:
  7.2 0.0 all-gather.4.cloned.1.call-start
  7.2 0.7 all-gather.4.cloned.1.call-update
  7.9 0.0 all-gather.6.cloned.1.call-start
  8.0 1.3 reduce_sum.9
  9.9 0.0 copy-start.5
  9.9 0.0 copy-start.6
  9.9 0.0 copy-start.7
  10.0 0.0 copy-start.8
  10.0 8.7 %conv_forward.1 = (bf16[8,21,4,16,640]{4,3,2,1,0:T(8,128)(2,1)}, f32[8,10,2,5,16,128]{5,4,3,2,1,0:T(8,128)}, f32[8,9,5,16,128]{4,3,2,1,0:T(8,128)}, f32[28,128,128]{2,1,0:T(8,128)S(1)}) custom-call(s32[4]{0:T(128)} %lengths_from.3, bf16[4,30,84,4,84]{4,3,2,1,0:T(4,128)(2,1)} %bitcast.38, f32[7896,128]{1,0:T(8,128)} %bitcast.33), custom_call_target="tpu_custom_call" | custom-call | tf_op jit(solution)/shard_map/conv_forward/pallas_call | solution.py:366
  18.7 0.1 pad_add_fusion
  18.7 12.1 %all-gather.4.cloned.1.call-done = f32[4,770,128]{2,1,0:T(8,128)} async-done(((f32[1,770,128]{2,1,0:T(8,128)}), f32[4,770,128]{2,1,0:T(8,128)}) %all-gather.4.cloned.1.call-update) | async-done | bytes 1576976 | tf_op jit(solution)/shard_map/all_gather | solution.py:1937
  30.8 0.0 copy-done.5
  30.8 0.0 copy-done.6
  30.8 0.0 copy-done.7
  30.8 0.0 copy-done.8
  30.8 41.8 %conditional.1 = ((f32[28,128,128]{2,1,0:T(8,128)}, f32[136,128]{1,0:T(8,128)}, f32[784,128]{1,0:T(8,128)}, f32[784,128]{1,0:T(8,128)}, f32[784,128]{1,0:T(8,128...) conditional(s32[]{:T(128)} %convert_element_type.3, ...), branch_computations={%region_1.0_spmd, %region_2.0_spmd} | conditional | bytes 8 | solution.py:1964
  38.6 30.7 %transformer_step_64.1 = (f32[28,128,128]{2,1,0:T(8,128)}, f32[136,128]{1,0:T(8,128)}, f32[784,128]{1,0:T(8,128)}, f32[784,128]{1,0:T(8,128)}, f32[784,128]{1,0:...) custom-call(s32[4]{0:T(128)S(1)} %get-tuple-element.73.lengths_from,, ...), custom_call_target="tpu_custom_call" | custom-call | tf_op jit(solution)/shard_map/cond/branch_1_fun/transformer_step_64/pallas_call | solution.py:1292
  72.6 0.0 all-gather.6.cloned.1.call-update
  72.6 0.5 collective-permute-start.2
  73.1 0.4 collective-permute-start.5
  73.5 6.6 %collective-permute-start.4 = (f32[808,128]{1,0:T(8,128)}, f32[808,128]{1,0:T(8,128)S(1)}, u32[]{:S(2)}, u32[]{:S(2)}) collective-permute-start(f32[808,128]{1,0:T(8,128)} %get-tuple-element.188), channel_id=1, source_target_pairs={{0,4},{1,5},{2,6},{3,7},{4,0},{5,1},{6,2},{7,3},{8,12},{9,13},{10,... | collective-permute-start | bytes 1241096 | tf_op jit(solution)/shard_map/ppermute | solution.py:2009
  80.1 0.0 collective-permute-start.3
  80.1 0.5 collective-permute-start.1
  80.6 0.5 collective-permute-done.2
  81.1 0.0 copy-start.4
  81.1 6.0 %collective-permute-start = (f32[784,128]{1,0:T(8,128)}, f32[784,128]{1,0:T(8,128)}, u32[]{:S(2)}, u32[]{:S(2)}) collective-permute-start(f32[784,128]{1,0:T(8,128)} %get-tuple-element.192), channel_id=1, source_target_pairs={{0,1},{1,0},{2,3},{3,2},{4,5},{5,4},{6,7},{7,6},{8,9},{9,8},{10,11... | collective-permute-start | bytes 1204232 | tf_op jit(solution)/shard_map/ppermute | solution.py:2003
  87.0 0.0 copy-done.4
  87.0 0.0 copy-start.3
  87.0 12.5 %conv_backward.1 = f32[616,128]{1,0:T(8,128)} custom-call(s32[4]{0:T(128)S(1)} %copy-done.5, bf16[8,21,4,16,640]{4,3,2,1,0:T(8,128)(2,1)} %get-tuple-element.130.picked_ref, f32[8,10,2,5,16,128]{5,4,3,2,1,0:T(8,128)} %get-tuple-element.131.z_one_ref, f32[8,9,5,16,128]{4,3,2,1,0:T(8,128)} %get-tuple-element.132.z_two_ref, ...), custom_call_target="tpu_custom_call" | custom-call | tf_op jit(solution)/shard_map/conv_backward/pallas_call | solution.py:675
  99.5 0.0 collective-permute-done.1
  99.5 0.0 collective-permute-done
  99.5 0.0 collective-permute-done.5
  99.5 0.0 copy-start
  99.6 0.0 collective-permute-done.4
  99.6 0.0 copy-start.1
  99.6 0.0 collective-permute-done.3
  99.6 0.0 copy-start.2
  99.6 0.7 copy-done
  100.3 0.1 copy-done.1
  100.4 0.1 copy-done.2
  100.6 0.0 copy-done.3
  100.6 73.0 %reduce_gradients.1 = (f32[469,8,128]{2,1,0:T(8,128)}, f32[12,8,128]{2,1,0:T(8,128)}, f32[98,8,128]{2,1,0:T(8,128)}, f32[8,128]{1,0:T(8,128)}) custom-call(f32[98,8,128]{2,1,0:T(8,128)} %bitcast.50, f32[98,8,128]{2,1,0:T(8,128)} %bitcast.6.refs_1_, f32[98,8,128]{2,1,0:T(8,128)} %bitcast.7.refs_2_, f32[98,8,128]{2,1,0:T(8,128)} %bitcast.49, ...), custom_call_target="tpu_custom_call" | custom-call | tf_op jit(solution)/shard_map/reduce_gradients/pallas_call | solution.py:1644
  173.6 0.0 all-gather.6.cloned.1.call-done.rows_ref
  173.6 20.1 %adam_update.1 = (f32[7896,128]{1,0:T(8,128)}, f32[7896,128]{1,0:T(8,128)}, f32[7896,128]{1,0:T(8,128)}, bf16[7896,128]{1,0:T(8,128)(2,1)}, f32[770,128]{1,0:T(8...) custom-call(f32[3752,128]{1,0:T(8,128)} %bitcast.41, ...), custom_call_target="tpu_custom_call" | custom-call | tf_op jit(solution)/shard_map/adam_update/pallas_call | solution.py:1865
Async XLA Ops:
  7.2 23.6 %all-gather.4.cloned.1.call-start = ((), (), s32[]{:S(2)}) async-start(), calls=%async_computation | async-start | bytes 1986560 | tf_op jit(solution)/shard_map/all_gather | solution.py:1937
  7.9 165.7 %all-gather.6.cloned.1.call-start = ((), (), s32[]{:S(2)}) async-start(), calls=%async_computation.1 | async-start | bytes 2297856 | tf_op jit(solution)/shard_map/all_gather | solution.py:1971
  9.9 20.9 %copy-start.5 = (s32[4]{0:T(128)S(1)}, s32[4]{0:T(128)}, u32[]{:S(2)}) copy-start(s32[4]{0:T(128)} %lengths_from.3) | copy-start | bytes 52
  9.9 20.9 %copy-start.6 = (f32[4,30]{1,0:T(4,128)S(1)}, f32[4,30]{1,0:T(4,128)}, u32[]{:S(2)}) copy-start(f32[4,30]{1,0:T(4,128)} %param.14) | copy-start | bytes 1444
  9.9 20.9 %copy-start.7 = (s32[4,30]{1,0:T(4,128)S(1)}, s32[4,30]{1,0:T(4,128)}, u32[]{:S(2)}) copy-start(s32[4,30]{1,0:T(4,128)} %param.15) | copy-start | bytes 1444
  10.0 20.9 %copy-start.8 = (s32[4]{0:T(128)S(1)}, s32[4]{0:T(128)}, u32[]{:S(2)}) copy-start(s32[4]{0:T(128)} %param.16) | copy-start | bytes 52
  72.6 8.5 %collective-permute-start.2 = (f32[784,128]{1,0:T(8,128)}, f32[784,128]{1,0:T(8,128)S(1)}, u32[]{:S(2)}, u32[]{:S(2)}) collective-permute-start(f32[784,128]{1,0:T(8,128)} %get-tuple-element.190), channel_id=1, source_target_pairs={{0,3},{1,2},{2,1},{3,0},{4,7},{5,6},{6,5},{7,4},{8,11},{9,10},{10,... | collective-permute-start | bytes 1204232 | tf_op jit(solution)/shard_map/ppermute | solution.py:2003
  73.1 26.4 %collective-permute-start.5 = (f32[808,128]{1,0:T(8,128)}, f32[808,128]{1,0:T(8,128)S(1)}, u32[]{:S(2)}, u32[]{:S(2)}) collective-permute-start(f32[808,128]{1,0:T(8,128)} %get-tuple-element.187), channel_id=1, source_target_pairs={{0,5},{1,4},{2,7},{3,6},{4,1},{5,0},{6,3},{7,2},{8,13},{9,12},{10,... | collective-permute-start | bytes 1241096 | tf_op jit(solution)/shard_map/ppermute | solution.py:2009
  73.5 26.0 %collective-permute-start.4 = (f32[808,128]{1,0:T(8,128)}, f32[808,128]{1,0:T(8,128)S(1)}, u32[]{:S(2)}, u32[]{:S(2)}) collective-permute-start(f32[808,128]{1,0:T(8,128)} %get-tuple-element.188), channel_id=1, source_target_pairs={{0,4},{1,5},{2,6},{3,7},{4,0},{5,1},{6,2},{7,3},{8,12},{9,13},{10,... | collective-permute-start | bytes 1241096 | tf_op jit(solution)/shard_map/ppermute | solution.py:2009
  80.1 19.5 %collective-permute-start.3 = (f32[808,128]{1,0:T(8,128)}, f32[808,128]{1,0:T(8,128)S(1)}, u32[]{:S(2)}, u32[]{:S(2)}) collective-permute-start(f32[808,128]{1,0:T(8,128)} %get-tuple-element.189), channel_id=1, source_target_pairs={{0,1},{1,0},{2,3},{3,2},{4,5},{5,4},{6,7},{7,6},{8,9},{9,8},{10,11... | collective-permute-start | bytes 1241096 | tf_op jit(solution)/shard_map/ppermute | solution.py:2009
  80.1 19.4 %collective-permute-start.1 = (f32[784,128]{1,0:T(8,128)}, f32[784,128]{1,0:T(8,128)}, u32[]{:S(2)}, u32[]{:S(2)}) collective-permute-start(f32[784,128]{1,0:T(8,128)} %get-tuple-element.191), channel_id=1, source_target_pairs={{0,2},{1,3},{2,0},{3,1},{4,6},{5,7},{6,4},{7,5},{8,10},{9,11},{10,... | collective-permute-start | bytes 1204232 | tf_op jit(solution)/shard_map/ppermute | solution.py:2003
  81.1 6.0 %copy-start.4 = (f32[784,128]{1,0:T(8,128)}, f32[784,128]{1,0:T(8,128)S(1)}, u32[]{:S(2)}) copy-start(f32[784,128]{1,0:T(8,128)S(1)} %collective-permute-done.2) | copy-start | bytes 1204228
  81.1 18.5 %collective-permute-start = (f32[784,128]{1,0:T(8,128)}, f32[784,128]{1,0:T(8,128)}, u32[]{:S(2)}, u32[]{:S(2)}) collective-permute-start(f32[784,128]{1,0:T(8,128)} %get-tuple-element.192), channel_id=1, source_target_pairs={{0,1},{1,0},{2,3},{3,2},{4,5},{5,4},{6,7},{7,6},{8,9},{9,8},{10,11... | collective-permute-start | bytes 1204232 | tf_op jit(solution)/shard_map/ppermute | solution.py:2003
  87.0 13.5 %copy-start.3 = (f32[808,128]{1,0:T(8,128)S(1)}, f32[808,128]{1,0:T(8,128)}, u32[]{:S(2)}) copy-start(f32[808,128]{1,0:T(8,128)} %get-tuple-element.185) | copy-start | bytes 1241092
  99.5 0.8 copy-start
  99.6 0.9 copy-start.1
  99.6 1.0 copy-start.2
Sparse Core Ops, SparseCore 0:
  9.6 21.1 all-gather.3
  72.7 63.8 all-gather.5
